TPU v7x, 32 devices: a whole 2x2x4 slice. The times are simulated.
32 devices in a mesh: row: 4 (over x, core), aux: 8 (over z, y).
Axes of the slice: x: 2, y: 2, z: 4, core: 2. Of those that a mesh axis runs over, the one named last changes fastest.
Arguments:
- tiles: bfloat16 [128, 1024, 256], P('aux', 'row'), may hold values from -6 to 6
- block_ids: int32 [4, 8, 2], P('row'), may hold values from 0 to 39, all different within a row
- coeffs: bfloat16 [5120, 256], P('row'), may hold values from -0.375 to 0.375
- energies: float32 [256], replicated, may hold values from -1.5 to -0.2
- tau: float32 [2], replicated, may hold values from 0.2 to 2
- weights: float32 [2], replicated, may hold values from 0.3 to 1.5
- coupling: bfloat16 [128, 128], replicated, may hold values from -0.5 to 0.5
Outputs:
- gamma: bfloat16 [1024, 128, 256], P(('row', 'aux'))
Inputs may be any that keep to these rules, and one draw needn't show every extreme that they name: `block_ids`: within one row slab and auxiliary slab the 2 block numbers differ; every block number is kept by some slab.
All inputs are finite; a program needn't handle non-finite values.
Results may differ from a plain program's by a relative error of at most 0.006.
Values may be sent and summed in bfloat16 or wider, within the bound.
No kernel may reach another device: no remote copies, remote signals or barrier semaphores. Data moves between devices by JAX's collectives and lax.ppermute only.
A program may use at most 64 MiB of HBM per device.

v0:
```python
import jax
import jax.numpy as jnp
from jax import lax
from jax.sharding import PartitionSpec as P

BLK = 128


def shards(tiles, block_ids, coeffs, energies, tau, weights, coupling):
    aux_count = lax.axis_size("aux")
    aux_here = lax.axis_index("aux")
    nu_width = block_ids.shape[2] * BLK
    occ_width = coeffs.shape[1]
    full_rows = lax.all_gather(coeffs, "row", axis=0, tiled=True)
    offsets = jnp.arange(BLK, dtype=jnp.int32)
    col_index = (block_ids[0][:, :, None] * BLK + offsets).reshape(aux_count, nu_width)
    picked = jnp.take(full_rows, col_index.reshape(-1), axis=0).reshape(
        aux_count, nu_width, occ_width
    )
    own_rows = lax.dynamic_index_in_dim(picked, aux_here, 0, keepdims=False)
    half_done = jnp.einsum(
        "pmk,ki->mpi", tiles, own_rows, preferred_element_type=jnp.float32
    ).astype(jnp.bfloat16)
    quadrature = jnp.sum(weights[:, None] * jnp.exp(tau[:, None] * energies[None, :]), axis=0)
    scaled = (picked.astype(jnp.float32) * quadrature).astype(jnp.bfloat16)
    mu_rows = half_done.shape[0]
    aux_dev = half_done.shape[1]
    sub_rows = mu_rows // aux_count
    stacked = half_done.reshape(aux_count, sub_rows, aux_dev, occ_width)
    received = lax.all_to_all(stacked, "aux", split_axis=0, concat_axis=2, tiled=True)[0]
    coupling_term = jnp.einsum(
        "qp,mpi->mqi", coupling, received, preferred_element_type=jnp.float32
    )
    coupled = (received.astype(jnp.float32) + coupling_term).astype(jnp.bfloat16)
    grouped = coupled.reshape(coupled.shape[0], aux_count, aux_dev, occ_width)
    gamma_out = jnp.einsum("masi,aki->mask", grouped, scaled, preferred_element_type=jnp.float32)
    return gamma_out.astype(jnp.bfloat16).reshape(coupled.shape[0], aux_count * aux_dev, nu_width)


def solution(mesh):
    in_specs = (P("aux", "row", None), P("row", None, None), P("row", None), P(), P(), P(), P())
    out_specs = P(("row", "aux"), None, None)
    return jax.shard_map(shards, mesh=mesh, in_specs=in_specs, out_specs=out_specs, check_vma=False)
```

profile of v0, /device:TPU:0, one launch (start us, length us, event | category | flops | bytes accessed | tf_op | source)
XLA Modules:
  0.0 118.2 jit_solution(10817392706426098826)
XLA Ops:
  6.5 0.0 copy-start
  6.5 0.0 all-gather.2.cloned.1.call-start
  6.5 0.7 all-gather.2.cloned.1.call-update
  7.3 0.7 multiply_bitcast_fusion
  7.9 0.1 copy.20
  8.0 0.1 fusion.13
  8.2 29.1 %all-gather.2.cloned.1.call-done = bf16[5120,256]{1,0:T(8,128)(2,1)} async-done(((bf16[1280,256]{1,0:T(8,128)(2,1)}), bf16[5120,256]{1,0:T(8,128)(2,1)}) %all-gather.2.cloned.1.call-update) | async-done | bytes 2621456 | tf_op jit(solution)/shard_map/all_gather | solution.py:14
  37.2 8.7 %gather_fusion = bf16[2048,256]{1,0:T(8,128)(2,1)S(1)} fusion(bf16[5120,256]{1,0:T(8,128)(2,1)} %all-gather.2.cloned.1.call-done, s32[2048]{0:T(1024)S(1)} %broadcast_clamp_fusion), kind=kCustom, calls=%fused_computation | custom fusion | bytes 2105344 | tf_op jit(solution)/shard_map/jit(_take)/gather | solution.py:17
  45.9 0.4 broadcast_select_fusion
  46.4 0.0 copy-done
  46.4 0.0 copy-start.1
  46.4 0.7 convolution_convert_fusion
  47.1 0.3 copy-done.1
  47.4 1.5 %copy.21 = bf16[8,32,16,256]{3,1,2,0:T(8,128)(2,1)} copy(bf16[8,32,16,256]{3,1,0,2:T(8,128)(2,1)S(1)} %bitcast.40) | data formatting | bytes 4194304 | tf_op jit(solution)/shard_map/reshape | solution.py:29
  48.9 5.6 %all-to-all-start = ((bf16[8,32,16,256]{3,1,2,0:T(8,128)(2,1)}), bf16[8,32,16,256]{3,1,2,0:T(8,128)(2,1)}, u32[]{:S(2)}, u32[]{:S(2)}) async-start(bf16[8,32,16,256]{3,1,2,0:T(8,128)(2,1)} %copy.21), calls=%async_computation | async-start | bytes 4194304 | tf_op jit(solution)/shard_map/all_to_all | solution.py:30
  54.6 0.1 multiply_reduce_fusion
  54.7 48.6 %all-to-all-done = bf16[8,32,16,256]{3,1,2,0:T(8,128)(2,1)} async-done(((bf16[8,32,16,256]{3,1,2,0:T(8,128)(2,1)}), bf16[8,32,16,256]{3,1,2,0:T(8,128)(2,1)}, u32[]{:S(2)}, u32[]{:S(2)}) %all-to-all-start) | async-done | bytes 2097184 | tf_op jit(solution)/shard_map/all_to_all | solution.py:30
  103.3 2.8 %copy.22 = bf16[1,32,8,16,256]{4,3,2,1,0:T(8,128)(2,1)S(1)} copy(bf16[1,32,8,16,256]{4,1,3,2,0:T(8,128)(2,1)} %bitcast.11) | data formatting | bytes 4194304 | tf_op jit(solution)/shard_map/all_to_all | solution.py:30
  106.1 0.0 copy-done.3
  106.1 0.0 copy-start.2
  106.1 0.7 fusion
  106.8 0.5 copy-done.2
  107.3 1.6 %fusion.3 = bf16[8,256,32,16]{1,2,3,0:T(8,128)(2,1)S(1)} fusion(bf16[32,8,16,256]{3,2,1,0:T(8,128)(2,1)S(1)} %bitcast.43, bf16[8,256,256]{2,1,0:T(8,128)(2,1)S(1)} %copy-done.2, f32[256]{0:T(256)S(1)} %multiply_reduce_fusion), kind=kOutput, calls=%fused_computation.6 | convolution fusion | flops 539492352 | bytes 5243904 | tf_op jit(solution)/shard_map/masi,aki->mask/dot_general | solution.py:36
  108.9 2.5 %copy.24 = bf16[32,128,256]{2,1,0:T(8,128)(2,1)} copy(bf16[32,128,256]{2,0,1:T(8,128)(2,1)S(1)} %bitcast.44) | data formatting | bytes 4194304 | tf_op jit(solution)/shard_map/reshape | solution.py:37
  (10 shorter events, 0.0 us)
Async XLA Ops:
  6.5 39.9 %copy-start = (bf16[16,256,256]{2,1,0:T(8,128)(2,1)S(1)}, bf16[16,256,256]{2,1,0:T(8,128)(2,1)}, u32[]{:S(2)}) copy-start(bf16[16,256,256]{2,1,0:T(8,128)(2,1)} %param.7) | copy-start | bytes 6291460
  6.5 30.7 %all-gather.2.cloned.1.call-start = ((), (), s32[]{:S(2)}) async-start(), calls=%async_computation.1 | async-start | bytes 3276800 | tf_op jit(solution)/shard_map/all_gather | solution.py:14
  46.4 1.0 copy-start.1
  48.9 5.7 %copy-start.4 = (f32[256]{0:T(256)S(1)}, f32[256]{0:T(256)}, u32[]{:S(2)}) copy-start(f32[256]{0:T(256)} %param.10) | copy-start | bytes 3076
  48.9 5.7 %copy-start.5 = (f32[2]{0:T(128)S(1)}, f32[2]{0:T(128)}, u32[]{:S(2)}) copy-start(f32[2]{0:T(128)} %param.12) | copy-start | bytes 28
  48.9 5.7 %copy-start.6 = (f32[2]{0:T(128)S(1)}, f32[2]{0:T(128)}, u32[]{:S(2)}) copy-start(f32[2]{0:T(128)} %param.11) | copy-start | bytes 28
  48.9 54.4 %all-to-all-start = ((bf16[8,32,16,256]{3,1,2,0:T(8,128)(2,1)}), bf16[8,32,16,256]{3,1,2,0:T(8,128)(2,1)}, u32[]{:S(2)}, u32[]{:S(2)}) async-start(bf16[8,32,16,256]{3,1,2,0:T(8,128)(2,1)} %copy.21), calls=%async_computation | async-start | bytes 4194304 | tf_op jit(solution)/shard_map/all_to_all | solution.py:30
  103.3 2.8 %copy-start.3 = (bf16[128,128]{1,0:T(8,128)(2,1)S(1)}, bf16[128,128]{1,0:T(8,128)(2,1)}, u32[]{:S(2)}) copy-start(bf16[128,128]{1,0:T(8,128)(2,1)} %param.13) | copy-start | bytes 98308
  106.1 1.2 %copy-start.2 = (bf16[8,256,256]{2,1,0:T(8,128)(2,1)S(1)}, bf16[8,256,256]{2,1,0:T(8,128)(2,1)}, u32[]{:S(2)}) copy-start(bf16[8,256,256]{2,1,0:T(8,128)(2,1)} %copy-done.1) | copy-start | bytes 3145732
Sparse Core Ops, SparseCore 0:
  8.9 28.2 all-gather.1
where the time goes:
time: 119 us; the launch traced here: 118 us
  waiting for transfers between devices  78.4 us (66%)
  local copies, waits for them, and re-layouts  16.4 us (14%)
  between operations  13.5 us (11%)
  starting transfers between devices  5.65 us (5%)
  matrix products  2.98 us (3%)
  other arithmetic  1.32 us (1%)
    all_to_all x1, waiting for transfers between devices, shards(): lax.all_to_all(stacked, 'aux', split_axis=0, concat_axis=2, tiled=True)[0]  48.6 us
    all_gather x1, waiting for transfers between devices, shards(): full_rows = lax.all_gather(coeffs, 'row', axis=0, tiled=True)  29.1 us
    gather x1, local copies, waits for them, and re-layouts, shards(): jnp.take(full_rows, col_index.reshape(-1), axis=0)  8.71 us
    all_to_all x1, starting transfers between devices, shards(): lax.all_to_all(stacked, 'aux', split_axis=0, concat_axis=2, tiled=True)[0]  5.65 us
    all_to_all x1, local copies, waits for them, and re-layouts, shards(): lax.all_to_all(stacked, 'aux', split_axis=0, concat_axis=2, tiled=True)[0]  2.77 us
    reshape x1, local copies, waits for them, and re-layouts, shards(): gamma_out.astype(jnp.bfloat16)  2.5 us
  transfers between devices with their start and end apart: 2, of which 2 were waited for; matrix products, arithmetic and copies ran while one was open for 1% of the time, Pallas kernels for 0%

commit v1 on v0

v1 whole, which is shorter than its diff:
```python
import functools
import math

import jax
import jax.numpy as jnp
from jax import lax
from jax.experimental import pallas as pl
from jax.experimental.pallas import tpu as pltpu
from jax.sharding import PartitionSpec as P

BLK = 128
FIRST = 2
SMEM = pl.BlockSpec(memory_space=pltpu.SMEM)
VMEM = pl.BlockSpec(memory_space=pltpu.VMEM)
ANY = pl.BlockSpec(memory_space=pl.ANY)
HBM = pl.BlockSpec(memory_space=pltpu.HBM)


def cost(flops, moved):
    return pl.CostEstimate(flops=flops, bytes_accessed=moved, transcendentals=0)


def swap(array, axis, bit, *after):
    if after:
        array = lax.optimization_barrier((array, *after))[0]
    return lax.ppermute(array, axis, [(i, i ^ bit) for i in range(lax.axis_size(axis))])


def cut_kernel(cuts, tiles_ref, *refs):
    count = len(cuts)
    out_refs, (held_ref, in_sems), to_hbm = refs[:count], refs[count : count + 2], refs[count + 2 :]
    sub = tiles_ref.shape[1] // lax.axis_size("aux")
    here = lax.axis_index("aux")
    copies = []
    for n, (k, first, rows) in enumerate(cuts):
        start = pl.multiple_of((here ^ k) * sub, sub) + first
        source = tiles_ref.at[:, pl.ds(start, rows), :]
        copies.append(pltpu.make_async_copy(source, held_ref.at[n, :, pl.ds(0, rows)], in_sems.at[n]))
        copies[-1].start()
    outs = []
    for n, (_, _, rows) in enumerate(cuts):
        copies[n].wait()
        turned = jnp.swapaxes(held_ref[n, :, :rows], 0, 1)
        if to_hbm:
            to_hbm[0][n, :rows] = turned
            outs.append(pltpu.make_async_copy(to_hbm[0].at[n, pl.ds(0, rows)], out_refs[n], to_hbm[1].at[n]))
            outs[-1].start()
        else:
            out_refs[n][...] = turned
    for copy in outs:
        copy.wait()


def cut_rows(tiles, cuts, to_hbm):
    aux_dev, _, width = tiles.shape
    count, most = len(cuts), max(rows for _, _, rows in cuts)
    scratch = [pltpu.VMEM((count, aux_dev, most, width), tiles.dtype), pltpu.SemaphoreType.DMA((count,))]
    if to_hbm:
        scratch += [pltpu.VMEM((count, most, aux_dev, width), tiles.dtype), pltpu.SemaphoreType.DMA((count,))]
    memory = pltpu.HBM if to_hbm else pltpu.VMEM
    return pl.pallas_call(
        functools.partial(cut_kernel, cuts),
        in_specs=[HBM],
        out_specs=[HBM if to_hbm else VMEM] * count,
        out_shape=[memory((rows, aux_dev, width), tiles.dtype) for _, _, rows in cuts],
        scratch_shapes=scratch,
        name="cut_rows",
        cost_estimate=cost(0, 4 * aux_dev * width * sum(rows for _, _, rows in cuts)),
        compiler_params=pltpu.CompilerParams(vmem_limit_bytes=24 * 2**20),
    )(tiles)


def pick_kernel(owners, ids_ref, energies_ref, tau_ref, weights_ref, *refs):
    held_refs, (picked_ref, scaled_ref, sems) = refs[:-3], refs[-3:]
    slabs, width, _ = picked_ref.shape
    rows = held_refs[0].shape[0]
    unit = math.gcd(rows, BLK)
    fine, per = BLK // unit, rows // unit
    here = lax.axis_index("row")

    def place(b):
        first = pl.multiple_of(b % (width // unit) * unit, unit)
        return picked_ref.at[b // (width // unit), pl.ds(first, unit)]

    def start(b, carry):
        block = b // fine
        piece = ids_ref[0, block % (width // BLK), block // (width // BLK)] * fine + b % fine
        first = pl.multiple_of(piece % per * unit, unit)
        for owner, held_ref in zip(owners, held_refs):
            @pl.when(piece // per == here ^ owner)
            def _():
                pltpu.make_async_copy(held_ref.at[pl.ds(first, unit)], place(b), sems.at[b]).start()
        return carry

    def end(b, carry):
        pltpu.make_async_copy(held_refs[0].at[pl.ds(0, unit)], place(b), sems.at[b]).wait()
        return carry

    lax.fori_loop(0, sems.shape[0], start, 0)
    lax.fori_loop(0, sems.shape[0], end, 0)
    quadrature = sum(weights_ref[t] * jnp.exp(tau_ref[t] * energies_ref[...]) for t in range(tau_ref.shape[0]))
    for a in range(slabs):
        block = picked_ref[a].astype(jnp.float32) * quadrature
        scaled_ref[a] = block.astype(jnp.bfloat16).T


def pick(held, owners, block_ids, energies, tau, weights):
    _, slabs, kept = block_ids.shape
    width, (rows, occ) = kept * BLK, held[0].shape
    return pl.pallas_call(
        functools.partial(pick_kernel, owners),
        in_specs=[SMEM, VMEM, SMEM, SMEM] + [ANY] * len(held),
        out_specs=[VMEM] * 2,
        out_shape=[
            jax.ShapeDtypeStruct((slabs, width, occ), jnp.bfloat16),
            jax.ShapeDtypeStruct((slabs, occ, width), jnp.bfloat16),
        ],
        scratch_shapes=[pltpu.SemaphoreType.DMA((slabs * width // math.gcd(rows, BLK),))],
        name="pick_and_scale",
        cost_estimate=cost(slabs * width * occ, 6 * slabs * width * occ),
        compiler_params=pltpu.CompilerParams(vmem_limit_bytes=24 * 2**20),
    )(jnp.swapaxes(block_ids, 1, 2), energies[None], tau, weights, *held)


def gamma_kernel(first, parts_first, slabs, *refs):
    parts, (picked_ref, scaled_ref, coupling_ref) = refs[:slabs], refs[slabs : slabs + 3]
    out_ref, half_ref, coupled_ref, gamma_ref, sems = refs[-5:]
    rows = half_ref.shape[0]
    _, aux_dev, width = parts[0].shape
    occ = picked_ref.shape[2]
    here = lax.axis_index("aux")
    for k, part in enumerate(parts):
        own = here ^ k
        mine = part[parts_first[k] : parts_first[k] + rows].reshape(rows * aux_dev, width)
        half = jnp.dot(mine, picked_ref[own], preferred_element_type=jnp.float32)
        half = half.astype(jnp.bfloat16).reshape(rows, aux_dev, occ)
        half_ref[:, pl.ds(pl.multiple_of(own * aux_dev, aux_dev), aux_dev), :] = half
    for m in range(rows):
        half = half_ref[m]
        term = jnp.dot(coupling_ref[...], half, preferred_element_type=jnp.float32)
        coupled_ref[m] = (half.astype(jnp.float32) + term).astype(jnp.bfloat16)
    copies = []
    for a in range(slabs):
        fns = pl.ds(a * aux_dev, aux_dev)
        gamma = jnp.dot(
            coupled_ref[:, fns, :].reshape(rows * aux_dev, occ), scaled_ref[a], preferred_element_type=jnp.float32
        )
        gamma_ref[:, fns, :] = gamma.astype(jnp.bfloat16).reshape(rows, aux_dev, width)
        target = out_ref.at[pl.ds(first, rows), fns, :]
        copies.append(pltpu.make_async_copy(gamma_ref.at[:, fns, :], target, sems.at[a]))
        copies[-1].start()
    for copy in copies:
        copy.wait()


def gamma_rows(first, rows, sub, parts, parts_first, picked, scaled, coupling, filled=None):
    slabs, width, occ = picked.shape
    aux_dev = parts[0].shape[1]
    fns = slabs * aux_dev
    operands = [*parts, picked, scaled, coupling]
    in_specs = [VMEM] * len(operands)
    aliases = {}
    if filled is not None:
        aliases = {len(operands): 0}
        operands.append(filled)
        in_specs.append(HBM)
    return pl.pallas_call(
        functools.partial(gamma_kernel, first, parts_first, slabs),
        in_specs=in_specs,
        out_specs=HBM,
        scratch_shapes=[
            pltpu.VMEM((rows, fns, occ), jnp.bfloat16),
            pltpu.VMEM((rows, fns, occ), jnp.bfloat16),
            pltpu.VMEM((rows, fns, width), jnp.bfloat16),
            pltpu.SemaphoreType.DMA((slabs,)),
        ],
        out_shape=jax.ShapeDtypeStruct((sub, fns, width), jnp.bfloat16),
        input_output_aliases=aliases,
        name="gamma_rows",
        cost_estimate=cost(2 * rows * fns * occ * (2 * width + fns), 8 * rows * fns * width + 2**21),
        compiler_params=pltpu.CompilerParams(vmem_limit_bytes=32 * 2**20),
    )(*operands)


def shards(tiles, block_ids, coeffs, energies, tau, weights, coupling):
    slabs = lax.axis_size("aux")
    sub = tiles.shape[1] // slabs
    far = slabs // 2
    cut = sub // 2
    chunks = ((0, cut), (cut, sub - cut))

    long = [(k, 0, sub) for k in range(far, slabs - 1)] + [(slabs - 1, *chunk) for chunk in chunks]
    short = [(k, 0, sub) for k in range(far - 1, -1, -1)]
    tiles = pltpu.with_memory_space_constraint(tiles, pltpu.HBM)
    pieces = cut_rows(tiles, long[:FIRST], False)
    *pieces, tiles, coeffs = lax.optimization_barrier((*pieces, tiles, coeffs))
    owners = range(lax.axis_size("row"))
    held = [swap(coeffs, "row", o) if o else coeffs for o in owners]
    tiles, _ = lax.optimization_barrier((tiles, held[1]))
    tiles = pltpu.with_memory_space_constraint(tiles, pltpu.HBM)
    pieces += cut_rows(tiles, long[FIRST:] + short, True)
    picked, scaled = pick(held, owners, block_ids, energies, tau, weights)

    parts = {short[-1]: pieces[-1]}
    for n, which in enumerate(short[:-1]):
        after = [] if n == 0 else [held[2]] if n == far - 2 else [parts[short[n - 1]]]
        parts[which] = swap(pieces[len(long) + n], "aux", which[0], *after)
    for n, which in enumerate(long):
        after = [parts[long[n - 2]]] if n >= 2 else []
        if n == len(long) - 1:
            after += [parts[long[n - 1]], picked]
        parts[which] = swap(pieces[n], "aux", which[0], *after)

    out = None
    for first, rows in chunks:
        which = [(k, first, rows) if k == slabs - 1 else (k, 0, sub) for k in range(slabs)]
        firsts = [0 if k == slabs - 1 else first for k in range(slabs)]
        out = gamma_rows(first, rows, sub, [parts[w] for w in which], firsts, picked, scaled, coupling, out)
    return out


def solution(mesh):
    in_specs = (P("aux", "row", None), P("row", None, None), P("row", None), P(), P(), P(), P())
    out_specs = P(("row", "aux"), None, None)
    return jax.shard_map(shards, mesh=mesh, in_specs=in_specs, out_specs=out_specs, check_vma=False)
```

time: 119 us -> 57.5 us (0.48)
  the two profiles are of different devices: /device:TPU:0 before, /device:TPU:17 now
where the time goes in v1:
time: 57.5 us; the launch traced here: 57.3 us
  waiting for transfers between devices  29.7 us (52%)
  starting transfers between devices  16.6 us (29%)
  Pallas kernels  10.8 us (19%)
    ppermute x11, waiting for transfers between devices, swap(): lax.ppermute(array, axis, [(i, i ^ bit) for i in range(lax.axis_size(axis...  29.7 us
    ppermute x11, starting transfers between devices, swap(): lax.ppermute(array, axis, [(i, i ^ bit) for i in range(lax.axis_size(axis...  16.6 us
    pallas_call x2, Pallas kernels, gamma_rows(): pl.pallas_call(functools.partial(gamma_kernel, first, parts_first, slabs)...  4.04 us
    pallas_call x2, Pallas kernels, cut_rows(): pl.pallas_call(functools.partial(cut_kernel, cuts), in_specs=[HBM], out_s...  3.47 us
    pallas_call x1, Pallas kernels, pick(): pl.pallas_call(functools.partial(pick_kernel, owners), in_specs=[SMEM, VM...  3.29 us
  transfers between devices with their start and end apart: 11, of which 5 were waited for; matrix products, arithmetic and copies ran while one was open for 0% of the time, Pallas kernels for 13%

profile of v1, /device:TPU:17, one launch (start us, length us, event | category | flops | bytes accessed | tf_op | source)
XLA Modules:
  0.0 57.3 jit_solution(8195144364705143029)
XLA Ops:
  0.0 1.2 %cut_rows.2 = (bf16[32,16,256]{2,1,0:T(8,128)(2,1)S(1)}, bf16[32,16,256]{2,1,0:T(8,128)(2,1)S(1)}) custom-call(bf16[16,256,256]{2,1,0:T(8,128)(2,1)} %tiles_ref.2), custom_call_target="tpu_custom_call" | custom-call | bytes 1048576 | tf_op jit(solution)/shard_map/cut_rows/pallas_call | solution.py:61
  1.2 0.0 copy-done.1
  1.2 0.7 %collective-permute-start = (bf16[1280,256]{1,0:T(8,128)(2,1)S(1)}, bf16[1280,256]{1,0:T(8,128)(2,1)S(1)}, u32[]{:S(2)}, u32[]{:S(2)}) collective-permute-start(bf16[1280,256]{1,0:T(8,128)(2,1)S(1)} %copy-done.1), channel_id=1, source_target_pairs={{0,8},{8,0},{16,24},{24,16},{1,9},{9,1},{17,25},{25,17},{2,10},{10... | collective-permute-start | bytes 1966088 | tf_op jit(solution)/shard_map/ppermute | solution.py:26
  2.0 1.2 %collective-permute-start.1 = (bf16[1280,256]{1,0:T(8,128)(2,1)S(1)}, bf16[1280,256]{1,0:T(8,128)(2,1)S(1)}, u32[]{:S(2)}, u32[]{:S(2)}) collective-permute-start(bf16[1280,256]{1,0:T(8,128)(2,1)S(1)} %copy-done.1), channel_id=1, source_target_pairs={{0,16},{8,24},{16,0},{24,8},{1,17},{9,25},{17,1},{25,9},{2,18},{10... | collective-permute-start | bytes 1966088 | tf_op jit(solution)/shard_map/ppermute | solution.py:26
  3.2 0.5 collective-permute-start.9
  3.7 0.0 collective-permute-start.5
  3.7 0.0 collective-permute-done.refs_1_
  3.7 2.3 %cut_rows.3 = (bf16[32,16,256]{2,1,0:T(8,128)(2,1)}, bf16[16,16,256]{2,1,0:T(8,128)(2,1)}, bf16[16,16,256]{2,1,0:T(8,128)(2,1)}, bf16[32,16,256]{2,1,0:T(8,128)(...) custom-call(bf16[16,256,256]{2,1,0:T(8,128)(2,1)} %tiles_ref.2), custom_call_target="tpu_custom_call" | custom-call | bytes 3145728 | tf_op jit(solution)/shard_map/cut_rows/pallas_call | solution.py:61
  6.0 2.4 %collective-permute-start.3 = (bf16[32,16,256]{2,1,0:T(8,128)(2,1)}, bf16[32,16,256]{2,1,0:T(8,128)(2,1)S(1)}, u32[]{:S(2)}, u32[]{:S(2)}) collective-permute-start(bf16[32,16,256]{2,1,0:T(8,128)(2,1)} %get-tuple-element.35), channel_id=1, source_target_pairs={{0,3},{1,2},{2,1},{3,0},{4,7},{5,6},{6,5},{7,4},{8,11},{9,10},{10,... | collective-permute-start | bytes 786440 | tf_op jit(solution)/shard_map/ppermute | solution.py:26
  8.4 2.3 %collective-permute-start.6 = (bf16[32,16,256]{2,1,0:T(8,128)(2,1)S(1)}, bf16[32,16,256]{2,1,0:T(8,128)(2,1)S(1)}, u32[]{:S(2)}, u32[]{:S(2)}) collective-permute-start(bf16[32,16,256]{2,1,0:T(8,128)(2,1)S(1)} %get-tuple-element.38), channel_id=1, source_target_pairs={{0,5},{1,4},{2,7},{3,6},{4,1},{5,0},{6,3},{7,2},{8,13},{9,12},{10,... | collective-permute-start | bytes 786440 | tf_op jit(solution)/shard_map/ppermute | solution.py:26
  10.6 4.5 %collective-permute-done.5.refs_4_ = bf16[32,16,256]{2,1,0:T(8,128)(2,1)S(1)} collective-permute-done((bf16[32,16,256]{2,1,0:T(8,128)(2,1)S(1)}, bf16[32,16,256]{2,1,0:T(8,128)(2,1)S(1)}, u32[]{:S(2)}, u32[]{:S(2)}) %collective-permute-start.5) | collective-permute-done | bytes 262176 | tf_op jit(solution)/shard_map/ppermute | solution.py:26
  15.1 2.7 %collective-permute-start.7 = (bf16[32,16,256]{2,1,0:T(8,128)(2,1)}, bf16[32,16,256]{2,1,0:T(8,128)(2,1)S(1)}, u32[]{:S(2)}, u32[]{:S(2)}) collective-permute-start(bf16[32,16,256]{2,1,0:T(8,128)(2,1)} %get-tuple-element.40), channel_id=1, source_target_pairs={{0,6},{1,7},{2,4},{3,5},{4,2},{5,3},{6,0},{7,1},{8,14},{9,15},{10,... | collective-permute-start | bytes 786440 | tf_op jit(solution)/shard_map/ppermute | solution.py:26
  17.8 0.5 collective-permute-done.1.refs_2_
  18.3 1.2 %collective-permute-start.2 = (bf16[32,16,256]{2,1,0:T(8,128)(2,1)}, bf16[32,16,256]{2,1,0:T(8,128)(2,1)S(1)}, u32[]{:S(2)}, u32[]{:S(2)}) collective-permute-start(bf16[32,16,256]{2,1,0:T(8,128)(2,1)} %get-tuple-element.33), channel_id=1, source_target_pairs={{0,1},{1,0},{2,3},{3,2},{4,5},{5,4},{6,7},{7,6},{8,9},{9,8},{10,11... | collective-permute-start | bytes 786440 | tf_op jit(solution)/shard_map/ppermute | solution.py:26
  19.5 0.0 collective-permute-done.3.refs_3_
  19.6 2.0 %collective-permute-start.4 = (bf16[32,16,256]{2,1,0:T(8,128)(2,1)}, bf16[32,16,256]{2,1,0:T(8,128)(2,1)S(1)}, u32[]{:S(2)}, u32[]{:S(2)}) collective-permute-start(bf16[32,16,256]{2,1,0:T(8,128)(2,1)} %get-tuple-element.36), channel_id=1, source_target_pairs={{0,2},{1,3},{2,0},{3,1},{4,6},{5,7},{6,4},{7,5},{8,10},{9,11},{10,... | collective-permute-start | bytes 786440 | tf_op jit(solution)/shard_map/ppermute | solution.py:26
  21.6 10.4 %collective-permute-done.6.refs_5_ = bf16[32,16,256]{2,1,0:T(8,128)(2,1)S(1)} collective-permute-done((bf16[32,16,256]{2,1,0:T(8,128)(2,1)S(1)}, bf16[32,16,256]{2,1,0:T(8,128)(2,1)S(1)}, u32[]{:S(2)}, u32[]{:S(2)}) %collective-permute-start.6) | collective-permute-done | bytes 262176 | tf_op jit(solution)/shard_map/ppermute | solution.py:26
  32.0 3.6 %collective-permute-start.8 = (bf16[16,16,256]{2,1,0:T(8,128)(2,1)}, bf16[16,16,256]{2,1,0:T(8,128)(2,1)S(1)}, u32[]{:S(2)}, u32[]{:S(2)}) collective-permute-start(bf16[16,16,256]{2,1,0:T(8,128)(2,1)} %get-tuple-element.43), channel_id=1, source_target_pairs={{0,7},{1,6},{2,5},{3,4},{4,3},{5,2},{6,1},{7,0},{8,15},{9,14},{10,... | collective-permute-start | bytes 393224 | tf_op jit(solution)/shard_map/ppermute | solution.py:26
  35.7 3.3 %pick_and_scale.1 = (bf16[8,256,256]{2,1,0:T(8,128)(2,1)S(1)}, bf16[8,256,256]{2,1,0:T(8,128)(2,1)S(1)}) custom-call(s32[1,2,8]{2,1,0:T(2,128)S(1)} %bitcast.2, f32[1,256]{1,0:T(1,128)S(1)} %bitcast.3, f32[2]{0:T(128)S(1)} %copy-done.5, f32[2]{0:T(128)S(1)} %copy-done.6, bf16[1280,256]{1,0:T(8,128)(2,1)S(1)} %copy-done.1, ...), custom_call_target="tpu_custom_call" | custom-call | flops 524288 | bytes 3145728 | tf_op jit(solution)/shard_map/pick_and_scale/pallas_call | solution.py:110
  39.0 8.6 %collective-permute-done.8.refs_7_ = bf16[16,16,256]{2,1,0:T(8,128)(2,1)S(1)} collective-permute-done((bf16[16,16,256]{2,1,0:T(8,128)(2,1)}, bf16[16,16,256]{2,1,0:T(8,128)(2,1)S(1)}, u32[]{:S(2)}, u32[]{:S(2)}) %collective-permute-start.8) | collective-permute-done | bytes 131104 | tf_op jit(solution)/shard_map/ppermute | solution.py:26
  47.6 0.0 collective-permute-done.7.refs_6_
  47.7 2.0 %gamma_rows.2.refs_11_ = bf16[32,128,256]{2,1,0:T(8,128)(2,1)} custom-call(bf16[32,16,256]{2,1,0:T(8,128)(2,1)S(1)} %copy-done, bf16[32,16,256]{2,1,0:T(8,128)(2,1)S(1)} %collective-permute-done.2.refs_1_, bf16[32,16,256]{2,1,0:T(8,128)(2,1)S(1)} %collective-permute-done.4.refs_2_, bf16[32,16,256]{2,1,0:T(8,128)(2,1)S(1)} %collective-permute-done.3.refs_3_, ...), custom_call_target="tpu_custom_call" | custom-call | flops 671088640 | bytes 6291456 | tf_op jit(solution)/shard_map/gamma_rows/pallas_call | solution.py:167
  49.7 5.6 %collective-permute-done.10.refs_7_ = bf16[16,16,256]{2,1,0:T(8,128)(2,1)S(1)} collective-permute-done((bf16[16,16,256]{2,1,0:T(8,128)(2,1)S(1)}, bf16[16,16,256]{2,1,0:T(8,128)(2,1)S(1)}, u32[]{:S(2)}, u32[]{:S(2)}) %collective-permute-start.10) | collective-permute-done | bytes 131104 | tf_op jit(solution)/shard_map/ppermute | solution.py:26
  55.3 2.0 %gamma_rows.3 = bf16[32,128,256]{2,1,0:T(8,128)(2,1)} custom-call(bf16[32,16,256]{2,1,0:T(8,128)(2,1)S(1)} %copy-done, bf16[32,16,256]{2,1,0:T(8,128)(2,1)S(1)} %collective-permute-done.2.refs_1_, bf16[32,16,256]{2,1,0:T(8,128)(2,1)S(1)} %collective-permute-done.4.refs_2_, ...), custom_call_target="tpu_custom_call", output_to_operand_aliasing={{}: (11, {})} | custom-call | flops 671088640 | bytes 6291456 | tf_op jit(solution)/shard_map/gamma_rows/pallas_call | solution.py:167
  (19 shorter events, 0.0 us)
Async XLA Ops:
  0.0 1.2 %copy-start.1 = (bf16[1280,256]{1,0:T(8,128)(2,1)S(1)}, bf16[1280,256]{1,0:T(8,128)(2,1)}, u32[]{:S(2)}) copy-start(bf16[1280,256]{1,0:T(8,128)(2,1)} %refs_0_) | copy-start | bytes 1966084
  0.0 35.6 %copy-start.6 = (f32[2]{0:T(128)S(1)}, f32[2]{0:T(128)}, u32[]{:S(2)}) copy-start(f32[2]{0:T(128)} %weights_ref.1) | copy-start | bytes 28
  0.0 35.6 %copy-start.5 = (f32[2]{0:T(128)S(1)}, f32[2]{0:T(128)}, u32[]{:S(2)}) copy-start(f32[2]{0:T(128)} %tau_ref.1) | copy-start | bytes 28
  0.0 35.6 %copy-start.4 = (f32[256]{0:T(256)S(1)}, f32[256]{0:T(256)}, u32[]{:S(2)}) copy-start(f32[256]{0:T(256)} %param.10) | copy-start | bytes 3076
  0.0 35.6 %copy-start.3 = (s32[1,8,2]{1,2,0:T(2,128)S(1)}, s32[1,8,2]{1,2,0:T(2,128)}, u32[]{:S(2)}) copy-start(s32[1,8,2]{1,2,0:T(2,128)} %param.8) | copy-start | bytes 196
  1.2 46.4 %copy-start.2 = (bf16[128,128]{1,0:T(8,128)(2,1)S(1)}, bf16[128,128]{1,0:T(8,128)(2,1)}, u32[]{:S(2)}) copy-start(bf16[128,128]{1,0:T(8,128)(2,1)} %refs_10_.3) | copy-start | bytes 98308
  1.2 2.5 %collective-permute-start = (bf16[1280,256]{1,0:T(8,128)(2,1)S(1)}, bf16[1280,256]{1,0:T(8,128)(2,1)S(1)}, u32[]{:S(2)}, u32[]{:S(2)}) collective-permute-start(bf16[1280,256]{1,0:T(8,128)(2,1)S(1)} %copy-done.1), channel_id=1, source_target_pairs={{0,8},{8,0},{16,24},{24,16},{1,9},{9,1},{17,25},{25,17},{2,10},{10... | collective-permute-start | bytes 1966088 | tf_op jit(solution)/shard_map/ppermute | solution.py:26
  2.0 16.3 %collective-permute-start.1 = (bf16[1280,256]{1,0:T(8,128)(2,1)S(1)}, bf16[1280,256]{1,0:T(8,128)(2,1)S(1)}, u32[]{:S(2)}, u32[]{:S(2)}) collective-permute-start(bf16[1280,256]{1,0:T(8,128)(2,1)S(1)} %copy-done.1), channel_id=1, source_target_pairs={{0,16},{8,24},{16,0},{24,8},{1,17},{9,25},{17,1},{25,9},{2,18},{10... | collective-permute-start | bytes 1966088 | tf_op jit(solution)/shard_map/ppermute | solution.py:26
  3.2 32.4 %collective-permute-start.9 = (bf16[1280,256]{1,0:T(8,128)(2,1)S(1)}, bf16[1280,256]{1,0:T(8,128)(2,1)S(1)}, u32[]{:S(2)}, u32[]{:S(2)}) collective-permute-start(bf16[1280,256]{1,0:T(8,128)(2,1)S(1)} %copy-done.1), channel_id=1, source_target_pairs={{0,24},{8,16},{16,8},{24,0},{1,25},{9,17},{17,9},{25,1},{2,26},{10... | collective-permute-start | bytes 1966088 | tf_op jit(solution)/shard_map/ppermute | solution.py:26
  3.7 11.4 %collective-permute-start.5 = (bf16[32,16,256]{2,1,0:T(8,128)(2,1)S(1)}, bf16[32,16,256]{2,1,0:T(8,128)(2,1)S(1)}, u32[]{:S(2)}, u32[]{:S(2)}) collective-permute-start(bf16[32,16,256]{2,1,0:T(8,128)(2,1)S(1)} %get-tuple-element.37), channel_id=1, source_target_pairs={{0,4},{1,5},{2,6},{3,7},{4,0},{5,1},{6,2},{7,3},{8,12},{9,13},{10,... | collective-permute-start | bytes 786440 | tf_op jit(solution)/shard_map/ppermute | solution.py:26
  6.0 41.6 %copy-start.7 = (bf16[16,16,256]{2,1,0:T(8,128)(2,1)S(1)}, bf16[16,16,256]{2,1,0:T(8,128)(2,1)}, u32[]{:S(2)}) copy-start(bf16[16,16,256]{2,1,0:T(8,128)(2,1)} %get-tuple-element.45) | copy-start | bytes 393220
  6.0 41.6 %copy-start = (bf16[32,16,256]{2,1,0:T(8,128)(2,1)S(1)}, bf16[32,16,256]{2,1,0:T(8,128)(2,1)}, u32[]{:S(2)}) copy-start(bf16[32,16,256]{2,1,0:T(8,128)(2,1)} %get-tuple-element.31.refs_0_) | copy-start | bytes 786436
  6.0 13.5 %collective-permute-start.3 = (bf16[32,16,256]{2,1,0:T(8,128)(2,1)}, bf16[32,16,256]{2,1,0:T(8,128)(2,1)S(1)}, u32[]{:S(2)}, u32[]{:S(2)}) collective-permute-start(bf16[32,16,256]{2,1,0:T(8,128)(2,1)} %get-tuple-element.35), channel_id=1, source_target_pairs={{0,3},{1,2},{2,1},{3,0},{4,7},{5,6},{6,5},{7,4},{8,11},{9,10},{10,... | collective-permute-start | bytes 786440 | tf_op jit(solution)/shard_map/ppermute | solution.py:26
  8.4 23.6 %collective-permute-start.6 = (bf16[32,16,256]{2,1,0:T(8,128)(2,1)S(1)}, bf16[32,16,256]{2,1,0:T(8,128)(2,1)S(1)}, u32[]{:S(2)}, u32[]{:S(2)}) collective-permute-start(bf16[32,16,256]{2,1,0:T(8,128)(2,1)S(1)} %get-tuple-element.38), channel_id=1, source_target_pairs={{0,5},{1,4},{2,7},{3,6},{4,1},{5,0},{6,3},{7,2},{8,13},{9,12},{10,... | collective-permute-start | bytes 786440 | tf_op jit(solution)/shard_map/ppermute | solution.py:26
  15.1 32.5 %collective-permute-start.7 = (bf16[32,16,256]{2,1,0:T(8,128)(2,1)}, bf16[32,16,256]{2,1,0:T(8,128)(2,1)S(1)}, u32[]{:S(2)}, u32[]{:S(2)}) collective-permute-start(bf16[32,16,256]{2,1,0:T(8,128)(2,1)} %get-tuple-element.40), channel_id=1, source_target_pairs={{0,6},{1,7},{2,4},{3,5},{4,2},{5,3},{6,0},{7,1},{8,14},{9,15},{10,... | collective-permute-start | bytes 786440 | tf_op jit(solution)/shard_map/ppermute | solution.py:26
  18.3 29.3 %collective-permute-start.2 = (bf16[32,16,256]{2,1,0:T(8,128)(2,1)}, bf16[32,16,256]{2,1,0:T(8,128)(2,1)S(1)}, u32[]{:S(2)}, u32[]{:S(2)}) collective-permute-start(bf16[32,16,256]{2,1,0:T(8,128)(2,1)} %get-tuple-element.33), channel_id=1, source_target_pairs={{0,1},{1,0},{2,3},{3,2},{4,5},{5,4},{6,7},{7,6},{8,9},{9,8},{10,11... | collective-permute-start | bytes 786440 | tf_op jit(solution)/shard_map/ppermute | solution.py:26
  19.6 28.1 %collective-permute-start.4 = (bf16[32,16,256]{2,1,0:T(8,128)(2,1)}, bf16[32,16,256]{2,1,0:T(8,128)(2,1)S(1)}, u32[]{:S(2)}, u32[]{:S(2)}) collective-permute-start(bf16[32,16,256]{2,1,0:T(8,128)(2,1)} %get-tuple-element.36), channel_id=1, source_target_pairs={{0,2},{1,3},{2,0},{3,1},{4,6},{5,7},{6,4},{7,5},{8,10},{9,11},{10,... | collective-permute-start | bytes 786440 | tf_op jit(solution)/shard_map/ppermute | solution.py:26
  32.0 15.6 %collective-permute-start.8 = (bf16[16,16,256]{2,1,0:T(8,128)(2,1)}, bf16[16,16,256]{2,1,0:T(8,128)(2,1)S(1)}, u32[]{:S(2)}, u32[]{:S(2)}) collective-permute-start(bf16[16,16,256]{2,1,0:T(8,128)(2,1)} %get-tuple-element.43), channel_id=1, source_target_pairs={{0,7},{1,6},{2,5},{3,4},{4,3},{5,2},{6,1},{7,0},{8,15},{9,14},{10,... | collective-permute-start | bytes 393224 | tf_op jit(solution)/shard_map/ppermute | solution.py:26
  47.6 7.7 %collective-permute-start.10 = (bf16[16,16,256]{2,1,0:T(8,128)(2,1)S(1)}, bf16[16,16,256]{2,1,0:T(8,128)(2,1)S(1)}, u32[]{:S(2)}, u32[]{:S(2)}) collective-permute-start(bf16[16,16,256]{2,1,0:T(8,128)(2,1)S(1)} %copy-done.7), channel_id=1, source_target_pairs={{0,7},{1,6},{2,5},{3,4},{4,3},{5,2},{6,1},{7,0},{8,15},{9,14},{10,... | collective-permute-start | bytes 393224 | tf_op jit(solution)/shard_map/ppermute | solution.py:26

commit v2 on v1

v2 whole, which is shorter than its diff:
```python
import functools
import math

import jax
import jax.numpy as jnp
from jax import lax
from jax.experimental import pallas as pl
from jax.experimental.pallas import tpu as pltpu
from jax.sharding import PartitionSpec as P

BLK = 128
SMEM = pl.BlockSpec(memory_space=pltpu.SMEM)
VMEM = pl.BlockSpec(memory_space=pltpu.VMEM)
ANY = pl.BlockSpec(memory_space=pl.ANY)
HBM = pl.BlockSpec(memory_space=pltpu.HBM)


def cost(flops, moved):
    return pl.CostEstimate(flops=flops, bytes_accessed=moved, transcendentals=0)


def params(mib):
    return pltpu.CompilerParams(vmem_limit_bytes=mib * 2**20)


def swap(array, axis, bit, *after):
    if after:
        array = lax.optimization_barrier((array, *after))[0]
    return lax.ppermute(array, axis, [(i, i ^ bit) for i in range(lax.axis_size(axis))])


def partner_rows(tiles_ref, k, first, rows):
    sub = tiles_ref.shape[1] // lax.axis_size("aux")
    start = pl.multiple_of((lax.axis_index("aux") ^ k) * sub, sub) + first
    return tiles_ref.at[:, pl.ds(start, rows), :]


def slice_kernel(ways, tiles_ref, out_ref, sems):
    copies = []
    for n, k in enumerate(ways):
        source = partner_rows(tiles_ref, k, 0, out_ref.shape[2])
        copies.append(pltpu.make_async_copy(source, out_ref.at[n], sems.at[n]))
        copies[-1].start()
    for copy in copies:
        copy.wait()


def slice_rows(tiles, ways, sub):
    aux_dev, _, width = tiles.shape
    shape = (len(ways), aux_dev, sub, width)
    return pl.pallas_call(
        functools.partial(slice_kernel, ways),
        in_specs=[HBM],
        out_specs=VMEM,
        out_shape=pltpu.VMEM(shape, tiles.dtype),
        scratch_shapes=[pltpu.SemaphoreType.DMA((len(ways),))],
        name="slice_rows",
        cost_estimate=cost(0, 4 * math.prod(shape)),
        compiler_params=params(4),
    )(tiles)


def turn_kernel(both_ref, *out_refs):
    for n, out_ref in enumerate(out_refs):
        out_ref[...] = jnp.swapaxes(both_ref[n], 0, 1)


def turn(both):
    count, aux_dev, sub, width = both.shape
    return pl.pallas_call(
        turn_kernel,
        in_specs=[VMEM],
        out_specs=[VMEM] * count,
        out_shape=[pltpu.VMEM((sub, aux_dev, width), both.dtype)] * count,
        name="turn",
        cost_estimate=cost(0, 4 * both.size),
        compiler_params=params(8),
    )(both)


def cut_kernel(cuts, tiles_ref, *refs):
    count = len(cuts)
    out_refs, (held_ref, turned_ref, in_sems, out_sems) = refs[:count], refs[count:]
    copies = []
    for n, (k, first, rows) in enumerate(cuts):
        source = partner_rows(tiles_ref, k, first, rows)
        copies.append(pltpu.make_async_copy(source, held_ref.at[n, :, pl.ds(0, rows)], in_sems.at[n]))
        copies[-1].start()
    outs = []
    for n, (_, _, rows) in enumerate(cuts):
        copies[n].wait()
        turned_ref[n, :rows] = jnp.swapaxes(held_ref[n, :, :rows], 0, 1)
        outs.append(pltpu.make_async_copy(turned_ref.at[n, pl.ds(0, rows)], out_refs[n], out_sems.at[n]))
        outs[-1].start()
    for copy in outs:
        copy.wait()


def cut_rows(tiles, cuts):
    aux_dev, _, width = tiles.shape
    count, most = len(cuts), max(rows for _, _, rows in cuts)
    return pl.pallas_call(
        functools.partial(cut_kernel, cuts),
        in_specs=[HBM],
        out_specs=[HBM] * count,
        out_shape=[pltpu.HBM((rows, aux_dev, width), tiles.dtype) for _, _, rows in cuts],
        scratch_shapes=[
            pltpu.VMEM((count, aux_dev, most, width), tiles.dtype),
            pltpu.VMEM((count, most, aux_dev, width), tiles.dtype),
            pltpu.SemaphoreType.DMA((count,)),
            pltpu.SemaphoreType.DMA((count,)),
        ],
        name="cut_rows",
        cost_estimate=cost(0, 4 * aux_dev * width * sum(rows for _, _, rows in cuts)),
        compiler_params=params(24),
    )(tiles)


def pick_kernel(owners, ids_ref, energies_ref, tau_ref, weights_ref, *refs):
    held_refs, (picked_ref, scaled_ref, sems) = refs[:-3], refs[-3:]
    slabs, width, _ = picked_ref.shape
    rows = held_refs[0].shape[0]
    unit = math.gcd(rows, BLK)
    fine, per = BLK // unit, rows // unit
    here = lax.axis_index("row")

    def place(b):
        first = pl.multiple_of(b % (width // unit) * unit, unit)
        return picked_ref.at[b // (width // unit), pl.ds(first, unit)]

    def start(b, carry):
        block = b // fine
        piece = ids_ref[0, block % (width // BLK), block // (width // BLK)] * fine + b % fine
        first = pl.multiple_of(piece % per * unit, unit)
        for owner, held_ref in zip(owners, held_refs):
            @pl.when(piece // per == here ^ owner)
            def _():
                pltpu.make_async_copy(held_ref.at[pl.ds(first, unit)], place(b), sems.at[b]).start()
        return carry

    def end(b, carry):
        pltpu.make_async_copy(held_refs[0].at[pl.ds(0, unit)], place(b), sems.at[b]).wait()
        return carry

    lax.fori_loop(0, sems.shape[0], start, 0)
    lax.fori_loop(0, sems.shape[0], end, 0)
    quadrature = sum(weights_ref[t] * jnp.exp(tau_ref[t] * energies_ref[...]) for t in range(tau_ref.shape[0]))
    for a in range(slabs):
        block = picked_ref[a].astype(jnp.float32) * quadrature
        scaled_ref[a] = block.astype(jnp.bfloat16).T


def pick(held, owners, block_ids, energies, tau, weights):
    _, slabs, kept = block_ids.shape
    width, (rows, occ) = kept * BLK, held[0].shape
    return pl.pallas_call(
        functools.partial(pick_kernel, owners),
        in_specs=[SMEM, VMEM, SMEM, SMEM] + [ANY] * len(held),
        out_specs=[VMEM] * 2,
        out_shape=[
            jax.ShapeDtypeStruct((slabs, width, occ), jnp.bfloat16),
            jax.ShapeDtypeStruct((slabs, occ, width), jnp.bfloat16),
        ],
        scratch_shapes=[pltpu.SemaphoreType.DMA((slabs * width // math.gcd(rows, BLK),))],
        name="pick_and_scale",
        cost_estimate=cost(slabs * width * occ, 6 * slabs * width * occ),
        compiler_params=params(24),
    )(jnp.swapaxes(block_ids, 1, 2), energies[None], tau, weights, *held)


def put_half(part, k, picked_ref, half_ref, first):
    rows, aux_dev, width = part.shape
    own = lax.axis_index("aux") ^ k
    half = jnp.dot(part.reshape(rows * aux_dev, width), picked_ref[own], preferred_element_type=jnp.float32)
    half = half.astype(jnp.bfloat16).reshape(rows, aux_dev, half.shape[-1])
    half_ref[first : first + rows, pl.ds(pl.multiple_of(own * aux_dev, aux_dev), aux_dev), :] = half


def half_kernel(*refs):
    for k, part_ref in enumerate(refs[:-2]):
        put_half(part_ref[...], k, refs[-2], refs[-1], 0)


def half_rows(parts, picked):
    slabs, width, occ = picked.shape
    rows, aux_dev, _ = parts[0].shape
    return pl.pallas_call(
        half_kernel,
        in_specs=[VMEM] * (len(parts) + 1),
        out_specs=VMEM,
        out_shape=pltpu.VMEM((rows, slabs * aux_dev, occ), jnp.bfloat16),
        name="half_rows",
        cost_estimate=cost(2 * len(parts) * rows * aux_dev * width * occ, 4 * len(parts) * rows * aux_dev * width),
        compiler_params=params(16),
    )(*parts, picked)


def gamma_kernel(first, aliased, last_ref, picked_ref, scaled_ref, coupling_ref, *refs):
    half_ref, out_ref, coupled_ref, gamma_ref, sems = refs[aliased:]
    rows, aux_dev, width = last_ref.shape
    slabs, occ, _ = scaled_ref.shape
    put_half(last_ref[...], slabs - 1, picked_ref, half_ref, first)
    for m in range(rows):
        half = half_ref[first + m]
        term = jnp.dot(coupling_ref[...], half, preferred_element_type=jnp.float32)
        coupled_ref[m] = (half.astype(jnp.float32) + term).astype(jnp.bfloat16)
    copies = []
    for a in range(slabs):
        fns = pl.ds(a * aux_dev, aux_dev)
        gamma = jnp.dot(
            coupled_ref[:, fns, :].reshape(rows * aux_dev, occ), scaled_ref[a], preferred_element_type=jnp.float32
        )
        gamma_ref[:, fns, :] = gamma.astype(jnp.bfloat16).reshape(rows, aux_dev, width)
        target = out_ref.at[pl.ds(first, rows), fns, :]
        copies.append(pltpu.make_async_copy(gamma_ref.at[:, fns, :], target, sems.at[a]))
        copies[-1].start()
    for copy in copies:
        copy.wait()


def gamma_rows(first, last, picked, scaled, coupling, half, filled=None):
    rows, aux_dev, width = last.shape
    sub, fns, occ = half.shape
    operands = [last, picked, scaled, coupling, half]
    in_specs, aliases = [VMEM] * 5, {4: 0}
    if filled is not None:
        aliases[len(operands)] = 1
        operands.append(filled)
        in_specs.append(HBM)
    return pl.pallas_call(
        functools.partial(gamma_kernel, first, len(aliases)),
        in_specs=in_specs,
        out_specs=[VMEM, HBM],
        out_shape=[pltpu.VMEM(half.shape, half.dtype), jax.ShapeDtypeStruct((sub, fns, width), jnp.bfloat16)],
        input_output_aliases=aliases,
        scratch_shapes=[
            pltpu.VMEM((rows, fns, occ), jnp.bfloat16),
            pltpu.VMEM((rows, fns, width), jnp.bfloat16),
            pltpu.SemaphoreType.DMA((scaled.shape[0],)),
        ],
        name="gamma_rows",
        cost_estimate=cost(2 * rows * fns * occ * (width + fns), 8 * rows * fns * width + 2**21),
        compiler_params=params(24),
    )(*operands)


def shards(tiles, block_ids, coeffs, energies, tau, weights, coupling):
    slabs = lax.axis_size("aux")
    sub = tiles.shape[1] // slabs
    far, cut = slabs // 2, sub // 2
    other = [(k, 0, sub) for k in range(far + 2, slabs - 1)]
    chunks = [(slabs - 1, 0, cut), (slabs - 1, cut, sub - cut)]
    near = [(k, 0, sub) for k in range(far - 1, -1, -1)]

    both = slice_rows(pltpu.with_memory_space_constraint(tiles, pltpu.HBM), (far, far + 1), sub)
    both, tiles, coeffs = lax.optimization_barrier((both, tiles, coeffs))
    owners = range(lax.axis_size("row"))
    held = [swap(coeffs, "row", o) if o else coeffs for o in owners]
    both = swap(both, "aux", far)
    tiles = lax.optimization_barrier((tiles, held[1]))[0]
    pieces = cut_rows(pltpu.with_memory_space_constraint(tiles, pltpu.HBM), [*other, *chunks, *near])
    pieces = dict(zip([*other, *chunks, *near], pieces))
    picked, scaled = pick(held, owners, block_ids, energies, tau, weights)

    parts = {near[-1]: pieces[near[-1]]}
    for n, which in enumerate(near[:-1]):
        after = [] if n == 0 else [held[2]] if n == 1 else [parts[near[n - 2]]]
        parts[which] = swap(pieces[which], "aux", which[0], *after)
    for n, which in enumerate(other):
        after = [held[1]] if n == 0 else [both] if n == 1 else [parts[other[n - 2]]]
        parts[which] = swap(pieces[which], "aux", which[0], *after)
    kept, passed = turn(both)
    parts[far, 0, sub], parts[far + 1, 0, sub] = kept, swap(passed, "aux", 1)
    early = swap(pieces[chunks[0]], "aux", slabs - 1, both)
    late = swap(pieces[chunks[1]], "aux", slabs - 1, parts[other[-1]], picked, *[parts[which] for which in near[1:-1]])

    half = half_rows([parts[k, 0, sub] for k in range(slabs - 1)], picked)
    half, out = gamma_rows(0, early, picked, scaled, coupling, half)
    return gamma_rows(cut, late, picked, scaled, coupling, half, out)[1]


def solution(mesh):
    in_specs = (P("aux", "row", None), P("row", None, None), P("row", None), P(), P(), P(), P())
    out_specs = P(("row", "aux"), None, None)
    return jax.shard_map(shards, mesh=mesh, in_specs=in_specs, out_specs=out_specs, check_vma=False)
```

time: 57.5 us -> 54.8 us (0.953)
  the two profiles are of different devices: /device:TPU:17 before, /device:TPU:0 now
where the time goes in v2:
time: 54.8 us; the launch traced here: 54.6 us
  starting transfers between devices  24.9 us (45%)
  waiting for transfers between devices  18.2 us (33%)
  Pallas kernels  11.2 us (20%)
    ppermute x11, starting transfers between devices, swap(): lax.ppermute(array, axis, [(i, i ^ bit) for i in range(lax.axis_size(axis...  24.9 us
    ppermute x11, waiting for transfers between devices, swap(): lax.ppermute(array, axis, [(i, i ^ bit) for i in range(lax.axis_size(axis...  18.2 us
    pallas_call x2, Pallas kernels, gamma_rows(): pl.pallas_call(functools.partial(gamma_kernel, first, len(aliases)), in_s...  3.66 us
    pallas_call x1, Pallas kernels, pick(): pl.pallas_call(functools.partial(pick_kernel, owners), in_specs=[SMEM, VM...  3.29 us
    pallas_call x1, Pallas kernels, cut_rows(): pl.pallas_call(functools.partial(cut_kernel, cuts), in_specs=[HBM], out_s...  2.3 us
    pallas_call x1, Pallas kernels, slice_rows(): pl.pallas_call(functools.partial(slice_kernel, ways), in_specs=[HBM], out...  1.12 us
  transfers between devices with their start and end apart: 11, of which 5 were waited for; matrix products, arithmetic and copies ran while one was open for 0% of the time, Pallas kernels for 15%

profile of v2, /device:TPU:0, one launch (start us, length us, event | category | flops | bytes accessed | tf_op | source)
XLA Modules:
  0.0 54.6 jit_solution(7656202007877862008)
XLA Ops:
  0.0 1.1 %slice_rows.1 = bf16[2,16,32,256]{3,2,1,0:T(8,128)(2,1)S(1)} custom-call(bf16[16,256,256]{2,1,0:T(8,128)(2,1)} %tiles_ref.2), custom_call_target="tpu_custom_call" | custom-call | bytes 1048576 | tf_op jit(solution)/shard_map/slice_rows/pallas_call | solution.py:51
  1.1 0.1 copy-done
  1.2 0.5 collective-permute-start
  1.7 2.5 %collective-permute-start.2 = (bf16[1280,256]{1,0:T(8,128)(2,1)S(1)}, bf16[1280,256]{1,0:T(8,128)(2,1)S(1)}, u32[]{:S(2)}, u32[]{:S(2)}) collective-permute-start(bf16[1280,256]{1,0:T(8,128)(2,1)S(1)} %copy-done), channel_id=1, source_target_pairs={{0,16},{8,24},{16,0},{24,8},{1,17},{9,25},{17,1},{25,9},{2,18},{10... | collective-permute-start | bytes 1966088 | tf_op jit(solution)/shard_map/ppermute | solution.py:29
  4.2 2.6 %collective-permute-start.8 = (bf16[2,16,32,256]{3,2,1,0:T(8,128)(2,1)S(1)}, bf16[2,16,32,256]{3,2,1,0:T(8,128)(2,1)S(1)}, u32[]{:S(2)}, u32[]{:S(2)}) collective-permute-start(bf16[2,16,32,256]{3,2,1,0:T(8,128)(2,1)S(1)} %slice_rows.1), channel_id=1, source_target_pairs={{0,4},{1,5},{2,6},{3,7},{4,0},{5,1},{6,2},{7,3},{8,12},{9,13},{10,... | collective-permute-start | bytes 1572872 | tf_op jit(solution)/shard_map/ppermute | solution.py:29
  6.8 0.0 collective-permute-start.3
  6.9 2.3 %cut_rows.1 = (bf16[32,16,256]{2,1,0:T(8,128)(2,1)}, bf16[16,16,256]{2,1,0:T(8,128)(2,1)}, bf16[16,16,256]{2,1,0:T(8,128)(2,1)}, bf16[32,16,256]{2,1,0:T(8,128)(...) custom-call(bf16[16,256,256]{2,1,0:T(8,128)(2,1)} %tiles_ref.2), custom_call_target="tpu_custom_call" | custom-call | bytes 3145728 | tf_op jit(solution)/shard_map/cut_rows/pallas_call | solution.py:102
  9.2 2.6 %collective-permute-start.5 = (bf16[32,16,256]{2,1,0:T(8,128)(2,1)}, bf16[32,16,256]{2,1,0:T(8,128)(2,1)S(1)}, u32[]{:S(2)}, u32[]{:S(2)}) collective-permute-start(bf16[32,16,256]{2,1,0:T(8,128)(2,1)} %get-tuple-element.38), channel_id=1, source_target_pairs={{0,3},{1,2},{2,1},{3,0},{4,7},{5,6},{6,5},{7,4},{8,11},{9,10},{10,... | collective-permute-start | bytes 786440 | tf_op jit(solution)/shard_map/ppermute | solution.py:29
  11.8 8.0 %collective-permute-done.2.refs_2_ = bf16[1280,256]{1,0:T(8,128)(2,1)S(1)} collective-permute-done((bf16[1280,256]{1,0:T(8,128)(2,1)S(1)}, bf16[1280,256]{1,0:T(8,128)(2,1)S(1)}, u32[]{:S(2)}, u32[]{:S(2)}) %collective-permute-start.2) | collective-permute-done | bytes 655392 | tf_op jit(solution)/shard_map/ppermute | solution.py:29
  19.8 2.0 %collective-permute-start.4 = (bf16[32,16,256]{2,1,0:T(8,128)(2,1)}, bf16[32,16,256]{2,1,0:T(8,128)(2,1)S(1)}, u32[]{:S(2)}, u32[]{:S(2)}) collective-permute-start(bf16[32,16,256]{2,1,0:T(8,128)(2,1)} %get-tuple-element.36), channel_id=1, source_target_pairs={{0,2},{1,3},{2,0},{3,1},{4,6},{5,7},{6,4},{7,5},{8,10},{9,11},{10,... | collective-permute-start | bytes 786440 | tf_op jit(solution)/shard_map/ppermute | solution.py:29
  21.9 2.5 %collective-permute-start.1 = (bf16[32,16,256]{2,1,0:T(8,128)(2,1)}, bf16[32,16,256]{2,1,0:T(8,128)(2,1)S(1)}, u32[]{:S(2)}, u32[]{:S(2)}) collective-permute-start(bf16[32,16,256]{2,1,0:T(8,128)(2,1)} %get-tuple-element.33), channel_id=1, source_target_pairs={{0,6},{1,7},{2,4},{3,5},{4,2},{5,3},{6,0},{7,1},{8,14},{9,15},{10,... | collective-permute-start | bytes 786440 | tf_op jit(solution)/shard_map/ppermute | solution.py:29
  24.3 0.5 collective-permute-done.5.refs_3_
  24.9 1.5 %collective-permute-start.6 = (bf16[32,16,256]{2,1,0:T(8,128)(2,1)}, bf16[32,16,256]{2,1,0:T(8,128)(2,1)S(1)}, u32[]{:S(2)}, u32[]{:S(2)}) collective-permute-start(bf16[32,16,256]{2,1,0:T(8,128)(2,1)} %get-tuple-element.39), channel_id=1, source_target_pairs={{0,1},{1,0},{2,3},{3,2},{4,5},{5,4},{6,7},{7,6},{8,9},{9,8},{10,11... | collective-permute-start | bytes 786440 | tf_op jit(solution)/shard_map/ppermute | solution.py:29
  26.4 5.3 %collective-permute-done.8.both_ref = bf16[2,16,32,256]{3,2,1,0:T(8,128)(2,1)S(1)} collective-permute-done((bf16[2,16,32,256]{3,2,1,0:T(8,128)(2,1)S(1)}, bf16[2,16,32,256]{3,2,1,0:T(8,128)(2,1)S(1)}, u32[]{:S(2)}, u32[]{:S(2)}) %collective-permute-start.8) | collective-permute-done | bytes 524320 | tf_op jit(solution)/shard_map/ppermute | solution.py:29
  31.7 0.1 turn.1
  31.8 1.6 %collective-permute-start.10 = (bf16[32,16,256]{2,1,0:T(8,128)(2,1)S(1)}, bf16[32,16,256]{2,1,0:T(8,128)(2,1)S(1)}, u32[]{:S(2)}, u32[]{:S(2)}) collective-permute-start(bf16[32,16,256]{2,1,0:T(8,128)(2,1)S(1)} %get-tuple-element.47), channel_id=1, source_target_pairs={{0,1},{1,0},{2,3},{3,2},{4,5},{5,4},{6,7},{7,6},{8,9},{9,8},{10,11... | collective-permute-start | bytes 786440 | tf_op jit(solution)/shard_map/ppermute | solution.py:29
  33.4 4.6 %collective-permute-start.9 = (bf16[16,16,256]{2,1,0:T(8,128)(2,1)}, bf16[16,16,256]{2,1,0:T(8,128)(2,1)S(1)}, u32[]{:S(2)}, u32[]{:S(2)}) collective-permute-start(bf16[16,16,256]{2,1,0:T(8,128)(2,1)} %get-tuple-element.44), channel_id=1, source_target_pairs={{0,7},{1,6},{2,5},{3,4},{4,3},{5,2},{6,1},{7,0},{8,15},{9,14},{10,... | collective-permute-start | bytes 393224 | tf_op jit(solution)/shard_map/ppermute | solution.py:29
  38.0 3.3 %pick_and_scale.1 = (bf16[8,256,256]{2,1,0:T(8,128)(2,1)S(1)}, bf16[8,256,256]{2,1,0:T(8,128)(2,1)S(1)}) custom-call(s32[1,2,8]{2,1,0:T(2,128)S(1)} %bitcast.2, f32[1,256]{1,0:T(1,128)S(1)} %bitcast.3, f32[2]{0:T(128)S(1)} %copy-done.5, f32[2]{0:T(128)S(1)} %copy-done.6, bf16[1280,256]{1,0:T(8,128)(2,1)S(1)} %copy-done, ...), custom_call_target="tpu_custom_call" | custom-call | flops 524288 | bytes 3145728 | tf_op jit(solution)/shard_map/pick_and_scale/pallas_call | solution.py:156
  41.3 3.1 %collective-permute-done.4.refs_2_ = bf16[32,16,256]{2,1,0:T(8,128)(2,1)S(1)} collective-permute-done((bf16[32,16,256]{2,1,0:T(8,128)(2,1)}, bf16[32,16,256]{2,1,0:T(8,128)(2,1)S(1)}, u32[]{:S(2)}, u32[]{:S(2)}) %collective-permute-start.4) | collective-permute-done | bytes 262176 | tf_op jit(solution)/shard_map/ppermute | solution.py:29
  44.4 4.5 %collective-permute-start.7 = (bf16[16,16,256]{2,1,0:T(8,128)(2,1)S(1)}, bf16[16,16,256]{2,1,0:T(8,128)(2,1)S(1)}, u32[]{:S(2)}, u32[]{:S(2)}) collective-permute-start(bf16[16,16,256]{2,1,0:T(8,128)(2,1)S(1)} %copy-done.7), channel_id=1, source_target_pairs={{0,7},{1,6},{2,5},{3,4},{4,3},{5,2},{6,1},{7,0},{8,15},{9,14},{10,... | collective-permute-start | bytes 393224 | tf_op jit(solution)/shard_map/ppermute | solution.py:29
  49.0 0.7 %half_rows.1.refs_0_ = bf16[32,128,256]{2,1,0:T(8,128)(2,1)S(1)} custom-call(bf16[32,16,256]{2,1,0:T(8,128)(2,1)S(1)} %copy-done.1, bf16[32,16,256]{2,1,0:T(8,128)(2,1)S(1)} %collective-permute-done.6.refs_1_, bf16[32,16,256]{2,1,0:T(8,128)(2,1)S(1)} %collective-permute-done.4.refs_2_, bf16[32,16,256]{2,1,0:T(8,128)(2,1)S(1)} %collective-permute-done.5.refs_3_, ...), custom_call_target="tpu_custom_call" | custom-call | flops 469762048 | bytes 3670016 | tf_op jit(solution)/shard_map/half_rows/pallas_call | solution.py:187
  49.7 1.8 %gamma_rows.2 = (bf16[32,128,256]{2,1,0:T(8,128)(2,1)S(1)}, bf16[32,128,256]{2,1,0:T(8,128)(2,1)}) custom-call(bf16[16,16,256]{2,1,0:T(8,128)(2,1)S(1)} %collective-permute-done.9.last_ref, bf16[8,256,256]{2,1,0:T(8,128)(2,1)S(1)} %get-tuple-element.34.refs_7_.picked_ref, ...), custom_call_target="tpu_custom_call", output_to_operand_aliasing={{0}: (4, {})} | custom-call | flops 402653184 | bytes 6291456 | tf_op jit(solution)/shard_map/gamma_rows/pallas_call | solution.py:230
  51.6 1.2 %collective-permute-done.7.last_ref = bf16[16,16,256]{2,1,0:T(8,128)(2,1)S(1)} collective-permute-done((bf16[16,16,256]{2,1,0:T(8,128)(2,1)S(1)}, bf16[16,16,256]{2,1,0:T(8,128)(2,1)S(1)}, u32[]{:S(2)}, u32[]{:S(2)}) %collective-permute-start.7) | collective-permute-done | bytes 131104 | tf_op jit(solution)/shard_map/ppermute | solution.py:29
  52.7 1.8 %gamma_rows.3 = (bf16[32,128,256]{2,1,0:T(8,128)(2,1)S(1)}, bf16[32,128,256]{2,1,0:T(8,128)(2,1)}) custom-call(bf16[16,16,256]{2,1,0:T(8,128)(2,1)S(1)} %collective-permute-done.7.last_ref, bf16[8,256,256]{2,1,0:T(8,128)(2,1)S(1)} %get-tuple-element.34.refs_7_.picked_ref, ...), custom_call_target="tpu_custom_call", output_to_operand_aliasing={{0}: (4, {}), {1}: (5, {})} | custom-call | flops 402653184 | bytes 6291456 | tf_op jit(solution)/shard_map/gamma_rows/pallas_call | solution.py:230
  (21 shorter events, 0.1 us)
Async XLA Ops:
  0.0 1.2 %copy-start = (bf16[1280,256]{1,0:T(8,128)(2,1)S(1)}, bf16[1280,256]{1,0:T(8,128)(2,1)}, u32[]{:S(2)}) copy-start(bf16[1280,256]{1,0:T(8,128)(2,1)} %refs_0_) | copy-start | bytes 1966084
  0.0 38.0 %copy-start.6 = (f32[2]{0:T(128)S(1)}, f32[2]{0:T(128)}, u32[]{:S(2)}) copy-start(f32[2]{0:T(128)} %weights_ref.1) | copy-start | bytes 28
  0.0 38.0 %copy-start.5 = (f32[2]{0:T(128)S(1)}, f32[2]{0:T(128)}, u32[]{:S(2)}) copy-start(f32[2]{0:T(128)} %tau_ref.1) | copy-start | bytes 28
  0.0 38.0 %copy-start.4 = (f32[256]{0:T(256)S(1)}, f32[256]{0:T(256)}, u32[]{:S(2)}) copy-start(f32[256]{0:T(256)} %param.10) | copy-start | bytes 3076
  0.0 38.0 %copy-start.3 = (s32[1,8,2]{1,2,0:T(2,128)S(1)}, s32[1,8,2]{1,2,0:T(2,128)}, u32[]{:S(2)}) copy-start(s32[1,8,2]{1,2,0:T(2,128)} %param.8) | copy-start | bytes 196
  1.2 5.6 %collective-permute-start = (bf16[1280,256]{1,0:T(8,128)(2,1)S(1)}, bf16[1280,256]{1,0:T(8,128)(2,1)S(1)}, u32[]{:S(2)}, u32[]{:S(2)}) collective-permute-start(bf16[1280,256]{1,0:T(8,128)(2,1)S(1)} %copy-done), channel_id=1, source_target_pairs={{0,8},{8,0},{16,24},{24,16},{1,9},{9,1},{17,25},{25,17},{2,10},{10... | collective-permute-start | bytes 1966088 | tf_op jit(solution)/shard_map/ppermute | solution.py:29
  1.7 18.1 %collective-permute-start.2 = (bf16[1280,256]{1,0:T(8,128)(2,1)S(1)}, bf16[1280,256]{1,0:T(8,128)(2,1)S(1)}, u32[]{:S(2)}, u32[]{:S(2)}) collective-permute-start(bf16[1280,256]{1,0:T(8,128)(2,1)S(1)} %copy-done), channel_id=1, source_target_pairs={{0,16},{8,24},{16,0},{24,8},{1,17},{9,25},{17,1},{25,9},{2,18},{10... | collective-permute-start | bytes 1966088 | tf_op jit(solution)/shard_map/ppermute | solution.py:29
  4.2 27.5 %collective-permute-start.8 = (bf16[2,16,32,256]{3,2,1,0:T(8,128)(2,1)S(1)}, bf16[2,16,32,256]{3,2,1,0:T(8,128)(2,1)S(1)}, u32[]{:S(2)}, u32[]{:S(2)}) collective-permute-start(bf16[2,16,32,256]{3,2,1,0:T(8,128)(2,1)S(1)} %slice_rows.1), channel_id=1, source_target_pairs={{0,4},{1,5},{2,6},{3,7},{4,0},{5,1},{6,2},{7,3},{8,12},{9,13},{10,... | collective-permute-start | bytes 1572872 | tf_op jit(solution)/shard_map/ppermute | solution.py:29
  6.8 26.6 %collective-permute-start.3 = (bf16[1280,256]{1,0:T(8,128)(2,1)S(1)}, bf16[1280,256]{1,0:T(8,128)(2,1)S(1)}, u32[]{:S(2)}, u32[]{:S(2)}) collective-permute-start(bf16[1280,256]{1,0:T(8,128)(2,1)S(1)} %copy-done), channel_id=1, source_target_pairs={{0,24},{8,16},{16,8},{24,0},{1,25},{9,17},{17,9},{25,1},{2,26},{10... | collective-permute-start | bytes 1966088 | tf_op jit(solution)/shard_map/ppermute | solution.py:29
  9.2 35.3 %copy-start.7 = (bf16[16,16,256]{2,1,0:T(8,128)(2,1)S(1)}, bf16[16,16,256]{2,1,0:T(8,128)(2,1)}, u32[]{:S(2)}) copy-start(bf16[16,16,256]{2,1,0:T(8,128)(2,1)} %get-tuple-element.40) | copy-start | bytes 393220
  9.2 39.8 %copy-start.1 = (bf16[32,16,256]{2,1,0:T(8,128)(2,1)S(1)}, bf16[32,16,256]{2,1,0:T(8,128)(2,1)}, u32[]{:S(2)}) copy-start(bf16[32,16,256]{2,1,0:T(8,128)(2,1)} %get-tuple-element.45.refs_0_) | copy-start | bytes 786436
  9.2 15.7 %collective-permute-start.5 = (bf16[32,16,256]{2,1,0:T(8,128)(2,1)}, bf16[32,16,256]{2,1,0:T(8,128)(2,1)S(1)}, u32[]{:S(2)}, u32[]{:S(2)}) collective-permute-start(bf16[32,16,256]{2,1,0:T(8,128)(2,1)} %get-tuple-element.38), channel_id=1, source_target_pairs={{0,3},{1,2},{2,1},{3,0},{4,7},{5,6},{6,5},{7,4},{8,11},{9,10},{10,... | collective-permute-start | bytes 786440 | tf_op jit(solution)/shard_map/ppermute | solution.py:29
  19.8 24.6 %collective-permute-start.4 = (bf16[32,16,256]{2,1,0:T(8,128)(2,1)}, bf16[32,16,256]{2,1,0:T(8,128)(2,1)S(1)}, u32[]{:S(2)}, u32[]{:S(2)}) collective-permute-start(bf16[32,16,256]{2,1,0:T(8,128)(2,1)} %get-tuple-element.36), channel_id=1, source_target_pairs={{0,2},{1,3},{2,0},{3,1},{4,6},{5,7},{6,4},{7,5},{8,10},{9,11},{10,... | collective-permute-start | bytes 786440 | tf_op jit(solution)/shard_map/ppermute | solution.py:29
  21.9 22.6 %collective-permute-start.1 = (bf16[32,16,256]{2,1,0:T(8,128)(2,1)}, bf16[32,16,256]{2,1,0:T(8,128)(2,1)S(1)}, u32[]{:S(2)}, u32[]{:S(2)}) collective-permute-start(bf16[32,16,256]{2,1,0:T(8,128)(2,1)} %get-tuple-element.33), channel_id=1, source_target_pairs={{0,6},{1,7},{2,4},{3,5},{4,2},{5,3},{6,0},{7,1},{8,14},{9,15},{10,... | collective-permute-start | bytes 786440 | tf_op jit(solution)/shard_map/ppermute | solution.py:29
  24.9 19.5 %collective-permute-start.6 = (bf16[32,16,256]{2,1,0:T(8,128)(2,1)}, bf16[32,16,256]{2,1,0:T(8,128)(2,1)S(1)}, u32[]{:S(2)}, u32[]{:S(2)}) collective-permute-start(bf16[32,16,256]{2,1,0:T(8,128)(2,1)} %get-tuple-element.39), channel_id=1, source_target_pairs={{0,1},{1,0},{2,3},{3,2},{4,5},{5,4},{6,7},{7,6},{8,9},{9,8},{10,11... | collective-permute-start | bytes 786440 | tf_op jit(solution)/shard_map/ppermute | solution.py:29
  31.8 17.1 %collective-permute-start.10 = (bf16[32,16,256]{2,1,0:T(8,128)(2,1)S(1)}, bf16[32,16,256]{2,1,0:T(8,128)(2,1)S(1)}, u32[]{:S(2)}, u32[]{:S(2)}) collective-permute-start(bf16[32,16,256]{2,1,0:T(8,128)(2,1)S(1)} %get-tuple-element.47), channel_id=1, source_target_pairs={{0,1},{1,0},{2,3},{3,2},{4,5},{5,4},{6,7},{7,6},{8,9},{9,8},{10,11... | collective-permute-start | bytes 786440 | tf_op jit(solution)/shard_map/ppermute | solution.py:29
  33.4 16.3 %collective-permute-start.9 = (bf16[16,16,256]{2,1,0:T(8,128)(2,1)}, bf16[16,16,256]{2,1,0:T(8,128)(2,1)S(1)}, u32[]{:S(2)}, u32[]{:S(2)}) collective-permute-start(bf16[16,16,256]{2,1,0:T(8,128)(2,1)} %get-tuple-element.44), channel_id=1, source_target_pairs={{0,7},{1,6},{2,5},{3,4},{4,3},{5,2},{6,1},{7,0},{8,15},{9,14},{10,... | collective-permute-start | bytes 393224 | tf_op jit(solution)/shard_map/ppermute | solution.py:29
  44.4 8.3 %collective-permute-start.7 = (bf16[16,16,256]{2,1,0:T(8,128)(2,1)S(1)}, bf16[16,16,256]{2,1,0:T(8,128)(2,1)S(1)}, u32[]{:S(2)}, u32[]{:S(2)}) collective-permute-start(bf16[16,16,256]{2,1,0:T(8,128)(2,1)S(1)} %copy-done.7), channel_id=1, source_target_pairs={{0,7},{1,6},{2,5},{3,4},{4,3},{5,2},{6,1},{7,0},{8,15},{9,14},{10,... | collective-permute-start | bytes 393224 | tf_op jit(solution)/shard_map/ppermute | solution.py:29
  49.0 0.8 %copy-start.2 = (bf16[128,128]{1,0:T(8,128)(2,1)S(1)}, bf16[128,128]{1,0:T(8,128)(2,1)}, u32[]{:S(2)}) copy-start(bf16[128,128]{1,0:T(8,128)(2,1)} %coupling_ref.3) | copy-start | bytes 98308

commit v3 on v2

--- a/solution.py
+++ b/solution.py
@@ -257,22 +257,21 @@
     owners = range(lax.axis_size("row"))
     held = [swap(coeffs, "row", o) if o else coeffs for o in owners]
     both = swap(both, "aux", far)
-    tiles = lax.optimization_barrier((tiles, held[1]))[0]
     pieces = cut_rows(pltpu.with_memory_space_constraint(tiles, pltpu.HBM), [*other, *chunks, *near])
     pieces = dict(zip([*other, *chunks, *near], pieces))
     picked, scaled = pick(held, owners, block_ids, energies, tau, weights)
 
     parts = {near[-1]: pieces[near[-1]]}
     for n, which in enumerate(near[:-1]):
-        after = [] if n == 0 else [held[2]] if n == 1 else [parts[near[n - 2]]]
+        after = [] if n == 0 else [parts[near[n - 1]]] if n < len(near) - 2 else [held[1]]
         parts[which] = swap(pieces[which], "aux", which[0], *after)
     for n, which in enumerate(other):
-        after = [held[1]] if n == 0 else [both] if n == 1 else [parts[other[n - 2]]]
+        after = [parts[near[-2]]] if n == 0 else [both] if n == 1 else [parts[other[n - 2]]]
         parts[which] = swap(pieces[which], "aux", which[0], *after)
     kept, passed = turn(both)
     parts[far, 0, sub], parts[far + 1, 0, sub] = kept, swap(passed, "aux", 1)
     early = swap(pieces[chunks[0]], "aux", slabs - 1, both)
-    late = swap(pieces[chunks[1]], "aux", slabs - 1, parts[other[-1]], picked, *[parts[which] for which in near[1:-1]])
+    late = swap(pieces[chunks[1]], "aux", slabs - 1, parts[other[-1]], picked)
 
     half = half_rows([parts[k, 0, sub] for k in range(slabs - 1)], picked)
     half, out = gamma_rows(0, early, picked, scaled, coupling, half)

time: 54.8 us -> 53.5 us (0.976)
  starting transfers between devices: 24.9 us -> 16.3 us
  waiting for transfers between devices: 18.2 us -> 25.1 us
    ppermute x11, starting transfers between devices: 24.9 us -> 16.3 us  [swap(): lax.ppermute(array, axis, [(i, i ^ bit) for i in range(lax.axis_size(axis...]
    ppermute x11, waiting for transfers between devices: 18.2 us -> 25.1 us  [swap(): lax.ppermute(array, axis, [(i, i ^ bit) for i in range(lax.axis_size(axis...]
  transfers between devices with their start and end apart: 11 -> 11, of which waited for: 5 -> 4; matrix products, arithmetic and copies ran while one was open for 0% -> 0% of each run, Pallas kernels for 15% -> 16%
where the time goes in v3:
time: 53.5 us; the launch traced here: 53 us
  waiting for transfers between devices  25.1 us (47%)
  starting transfers between devices  16.3 us (30%)
  Pallas kernels  11.2 us (21%)
    ppermute x11, waiting for transfers between devices, swap(): lax.ppermute(array, axis, [(i, i ^ bit) for i in range(lax.axis_size(axis...  25.1 us
    ppermute x11, starting transfers between devices, swap(): lax.ppermute(array, axis, [(i, i ^ bit) for i in range(lax.axis_size(axis...  16.3 us
    pallas_call x2, Pallas kernels, gamma_rows(): pl.pallas_call(functools.partial(gamma_kernel, first, len(aliases)), in_s...  3.66 us
    pallas_call x1, Pallas kernels, pick(): pl.pallas_call(functools.partial(pick_kernel, owners), in_specs=[SMEM, VM...  3.29 us
    pallas_call x1, Pallas kernels, cut_rows(): pl.pallas_call(functools.partial(cut_kernel, cuts), in_specs=[HBM], out_s...  2.3 us
    pallas_call x1, Pallas kernels, slice_rows(): pl.pallas_call(functools.partial(slice_kernel, ways), in_specs=[HBM], out...  1.12 us
  transfers between devices with their start and end apart: 11, of which 4 were waited for; matrix products, arithmetic and copies ran while one was open for 0% of the time, Pallas kernels for 16%

profile of v3, /device:TPU:0, one launch (start us, length us, event | category | flops | bytes accessed | tf_op | source)
XLA Modules:
  0.0 53.0 jit_solution(3382131967021975787)
XLA Ops:
  0.0 1.1 %slice_rows.1 = bf16[2,16,32,256]{3,2,1,0:T(8,128)(2,1)S(1)} custom-call(bf16[16,256,256]{2,1,0:T(8,128)(2,1)} %tiles_ref.2), custom_call_target="tpu_custom_call" | custom-call | bytes 1048576 | tf_op jit(solution)/shard_map/slice_rows/pallas_call | solution.py:51
  1.1 0.1 copy-done
  1.2 0.5 collective-permute-start
  1.7 3.6 %collective-permute-start.6 = (bf16[2,16,32,256]{3,2,1,0:T(8,128)(2,1)S(1)}, bf16[2,16,32,256]{3,2,1,0:T(8,128)(2,1)S(1)}, u32[]{:S(2)}, u32[]{:S(2)}) collective-permute-start(bf16[2,16,32,256]{3,2,1,0:T(8,128)(2,1)S(1)} %slice_rows.1), channel_id=1, source_target_pairs={{0,4},{1,5},{2,6},{3,7},{4,0},{5,1},{6,2},{7,3},{8,12},{9,13},{10,... | collective-permute-start | bytes 1572872 | tf_op jit(solution)/shard_map/ppermute | solution.py:29
  5.3 1.3 %collective-permute-start.4 = (bf16[1280,256]{1,0:T(8,128)(2,1)S(1)}, bf16[1280,256]{1,0:T(8,128)(2,1)S(1)}, u32[]{:S(2)}, u32[]{:S(2)}) collective-permute-start(bf16[1280,256]{1,0:T(8,128)(2,1)S(1)} %copy-done), channel_id=1, source_target_pairs={{0,24},{8,16},{16,8},{24,0},{1,25},{9,17},{17,9},{25,1},{2,26},{10... | collective-permute-start | bytes 1966088 | tf_op jit(solution)/shard_map/ppermute | solution.py:29
  6.6 0.5 %collective-permute-start.3 = (bf16[1280,256]{1,0:T(8,128)(2,1)S(1)}, bf16[1280,256]{1,0:T(8,128)(2,1)S(1)}, u32[]{:S(2)}, u32[]{:S(2)}) collective-permute-start(bf16[1280,256]{1,0:T(8,128)(2,1)S(1)} %copy-done), channel_id=1, source_target_pairs={{0,16},{8,24},{16,0},{24,8},{1,17},{9,25},{17,1},{25,9},{2,18},{10... | collective-permute-start | bytes 1966088 | tf_op jit(solution)/shard_map/ppermute | solution.py:29
  7.1 2.3 %cut_rows.1 = (bf16[32,16,256]{2,1,0:T(8,128)(2,1)}, bf16[16,16,256]{2,1,0:T(8,128)(2,1)}, bf16[16,16,256]{2,1,0:T(8,128)(2,1)}, bf16[32,16,256]{2,1,0:T(8,128)(...) custom-call(bf16[16,256,256]{2,1,0:T(8,128)(2,1)} %tiles_ref.2), custom_call_target="tpu_custom_call" | custom-call | bytes 3145728 | tf_op jit(solution)/shard_map/cut_rows/pallas_call | solution.py:102
  9.5 1.6 %collective-permute-start.1 = (bf16[32,16,256]{2,1,0:T(8,128)(2,1)}, bf16[32,16,256]{2,1,0:T(8,128)(2,1)S(1)}, u32[]{:S(2)}, u32[]{:S(2)}) collective-permute-start(bf16[32,16,256]{2,1,0:T(8,128)(2,1)} %get-tuple-element.32), channel_id=1, source_target_pairs={{0,1},{1,0},{2,3},{3,2},{4,5},{5,4},{6,7},{7,6},{8,9},{9,8},{10,11... | collective-permute-start | bytes 786440 | tf_op jit(solution)/shard_map/ppermute | solution.py:29
  11.1 1.5 %collective-permute-start.8 = (bf16[32,16,256]{2,1,0:T(8,128)(2,1)}, bf16[32,16,256]{2,1,0:T(8,128)(2,1)S(1)}, u32[]{:S(2)}, u32[]{:S(2)}) collective-permute-start(bf16[32,16,256]{2,1,0:T(8,128)(2,1)} %get-tuple-element.42), channel_id=1, source_target_pairs={{0,3},{1,2},{2,1},{3,0},{4,7},{5,6},{6,5},{7,4},{8,11},{9,10},{10,... | collective-permute-start | bytes 786440 | tf_op jit(solution)/shard_map/ppermute | solution.py:29
  12.6 10.9 %collective-permute-done.1.refs_1_ = bf16[32,16,256]{2,1,0:T(8,128)(2,1)S(1)} collective-permute-done((bf16[32,16,256]{2,1,0:T(8,128)(2,1)}, bf16[32,16,256]{2,1,0:T(8,128)(2,1)S(1)}, u32[]{:S(2)}, u32[]{:S(2)}) %collective-permute-start.1) | collective-permute-done | bytes 262176 | tf_op jit(solution)/shard_map/ppermute | solution.py:29
  23.5 1.5 %collective-permute-start.2 = (bf16[32,16,256]{2,1,0:T(8,128)(2,1)}, bf16[32,16,256]{2,1,0:T(8,128)(2,1)S(1)}, u32[]{:S(2)}, u32[]{:S(2)}) collective-permute-start(bf16[32,16,256]{2,1,0:T(8,128)(2,1)} %get-tuple-element.33), channel_id=1, source_target_pairs={{0,6},{1,7},{2,4},{3,5},{4,2},{5,3},{6,0},{7,1},{8,14},{9,15},{10,... | collective-permute-start | bytes 786440 | tf_op jit(solution)/shard_map/ppermute | solution.py:29
  25.0 10.8 %collective-permute-done.8.refs_3_ = bf16[32,16,256]{2,1,0:T(8,128)(2,1)S(1)} collective-permute-done((bf16[32,16,256]{2,1,0:T(8,128)(2,1)}, bf16[32,16,256]{2,1,0:T(8,128)(2,1)S(1)}, u32[]{:S(2)}, u32[]{:S(2)}) %collective-permute-start.8) | collective-permute-done | bytes 262176 | tf_op jit(solution)/shard_map/ppermute | solution.py:29
  35.8 0.1 turn.1
  35.9 1.1 %collective-permute-start.10 = (bf16[32,16,256]{2,1,0:T(8,128)(2,1)S(1)}, bf16[32,16,256]{2,1,0:T(8,128)(2,1)S(1)}, u32[]{:S(2)}, u32[]{:S(2)}) collective-permute-start(bf16[32,16,256]{2,1,0:T(8,128)(2,1)S(1)} %get-tuple-element.45), channel_id=1, source_target_pairs={{0,1},{1,0},{2,3},{3,2},{4,5},{5,4},{6,7},{7,6},{8,9},{9,8},{10,11... | collective-permute-start | bytes 786440 | tf_op jit(solution)/shard_map/ppermute | solution.py:29
  37.0 3.0 %collective-permute-start.7 = (bf16[16,16,256]{2,1,0:T(8,128)(2,1)}, bf16[16,16,256]{2,1,0:T(8,128)(2,1)S(1)}, u32[]{:S(2)}, u32[]{:S(2)}) collective-permute-start(bf16[16,16,256]{2,1,0:T(8,128)(2,1)} %get-tuple-element.39), channel_id=1, source_target_pairs={{0,7},{1,6},{2,5},{3,4},{4,3},{5,2},{6,1},{7,0},{8,15},{9,14},{10,... | collective-permute-start | bytes 393224 | tf_op jit(solution)/shard_map/ppermute | solution.py:29
  40.1 3.3 %pick_and_scale.1 = (bf16[8,256,256]{2,1,0:T(8,128)(2,1)S(1)}, bf16[8,256,256]{2,1,0:T(8,128)(2,1)S(1)}) custom-call(s32[1,2,8]{2,1,0:T(2,128)S(1)} %bitcast.2, f32[1,256]{1,0:T(1,128)S(1)} %bitcast.3, f32[2]{0:T(128)S(1)} %copy-done.5, f32[2]{0:T(128)S(1)} %copy-done.6, bf16[1280,256]{1,0:T(8,128)(2,1)S(1)} %copy-done, ...), custom_call_target="tpu_custom_call" | custom-call | flops 524288 | bytes 3145728 | tf_op jit(solution)/shard_map/pick_and_scale/pallas_call | solution.py:156
  43.4 1.7 %collective-permute-start.5 = (bf16[16,16,256]{2,1,0:T(8,128)(2,1)S(1)}, bf16[16,16,256]{2,1,0:T(8,128)(2,1)S(1)}, u32[]{:S(2)}, u32[]{:S(2)}) collective-permute-start(bf16[16,16,256]{2,1,0:T(8,128)(2,1)S(1)} %copy-done.7), channel_id=1, source_target_pairs={{0,7},{1,6},{2,5},{3,4},{4,3},{5,2},{6,1},{7,0},{8,15},{9,14},{10,... | collective-permute-start | bytes 393224 | tf_op jit(solution)/shard_map/ppermute | solution.py:29
  45.1 0.0 collective-permute-done.9.refs_2_
  45.1 0.4 collective-permute-done.10.refs_5_
  45.6 0.7 %half_rows.1.refs_0_ = bf16[32,128,256]{2,1,0:T(8,128)(2,1)S(1)} custom-call(bf16[32,16,256]{2,1,0:T(8,128)(2,1)S(1)} %copy-done.1, bf16[32,16,256]{2,1,0:T(8,128)(2,1)S(1)} %collective-permute-done.1.refs_1_, bf16[32,16,256]{2,1,0:T(8,128)(2,1)S(1)} %collective-permute-done.9.refs_2_, bf16[32,16,256]{2,1,0:T(8,128)(2,1)S(1)} %collective-permute-done.8.refs_3_, ...), custom_call_target="tpu_custom_call" | custom-call | flops 469762048 | bytes 3670016 | tf_op jit(solution)/shard_map/half_rows/pallas_call | solution.py:187
  46.3 0.0 copy-done.2
  46.4 1.8 %gamma_rows.2 = (bf16[32,128,256]{2,1,0:T(8,128)(2,1)S(1)}, bf16[32,128,256]{2,1,0:T(8,128)(2,1)}) custom-call(bf16[16,16,256]{2,1,0:T(8,128)(2,1)S(1)} %collective-permute-done.7.last_ref, bf16[8,256,256]{2,1,0:T(8,128)(2,1)S(1)} %get-tuple-element.34.refs_7_.picked_ref, ...), custom_call_target="tpu_custom_call", output_to_operand_aliasing={{0}: (4, {})} | custom-call | flops 402653184 | bytes 6291456 | tf_op jit(solution)/shard_map/gamma_rows/pallas_call | solution.py:230
  48.2 2.9 %collective-permute-done.5.last_ref = bf16[16,16,256]{2,1,0:T(8,128)(2,1)S(1)} collective-permute-done((bf16[16,16,256]{2,1,0:T(8,128)(2,1)S(1)}, bf16[16,16,256]{2,1,0:T(8,128)(2,1)S(1)}, u32[]{:S(2)}, u32[]{:S(2)}) %collective-permute-start.5) | collective-permute-done | bytes 131104 | tf_op jit(solution)/shard_map/ppermute | solution.py:29
  51.1 1.8 %gamma_rows.3 = (bf16[32,128,256]{2,1,0:T(8,128)(2,1)S(1)}, bf16[32,128,256]{2,1,0:T(8,128)(2,1)}) custom-call(bf16[16,16,256]{2,1,0:T(8,128)(2,1)S(1)} %collective-permute-done.5.last_ref, bf16[8,256,256]{2,1,0:T(8,128)(2,1)S(1)} %get-tuple-element.34.refs_7_.picked_ref, ...), custom_call_target="tpu_custom_call", output_to_operand_aliasing={{0}: (4, {}), {1}: (5, {})} | custom-call | flops 402653184 | bytes 6291456 | tf_op jit(solution)/shard_map/gamma_rows/pallas_call | solution.py:230
  (21 shorter events, 0.0 us)
Async XLA Ops:
  0.0 1.2 %copy-start = (bf16[1280,256]{1,0:T(8,128)(2,1)S(1)}, bf16[1280,256]{1,0:T(8,128)(2,1)}, u32[]{:S(2)}) copy-start(bf16[1280,256]{1,0:T(8,128)(2,1)} %refs_0_) | copy-start | bytes 1966084
  0.0 40.0 %copy-start.6 = (f32[2]{0:T(128)S(1)}, f32[2]{0:T(128)}, u32[]{:S(2)}) copy-start(f32[2]{0:T(128)} %weights_ref.1) | copy-start | bytes 28
  0.0 40.0 %copy-start.5 = (f32[2]{0:T(128)S(1)}, f32[2]{0:T(128)}, u32[]{:S(2)}) copy-start(f32[2]{0:T(128)} %tau_ref.1) | copy-start | bytes 28
  0.0 40.0 %copy-start.4 = (f32[256]{0:T(256)S(1)}, f32[256]{0:T(256)}, u32[]{:S(2)}) copy-start(f32[256]{0:T(256)} %param.10) | copy-start | bytes 3076
  0.0 40.1 %copy-start.3 = (s32[1,8,2]{1,2,0:T(2,128)S(1)}, s32[1,8,2]{1,2,0:T(2,128)}, u32[]{:S(2)}) copy-start(s32[1,8,2]{1,2,0:T(2,128)} %param.8) | copy-start | bytes 196
  1.2 8.2 %collective-permute-start = (bf16[1280,256]{1,0:T(8,128)(2,1)S(1)}, bf16[1280,256]{1,0:T(8,128)(2,1)S(1)}, u32[]{:S(2)}, u32[]{:S(2)}) collective-permute-start(bf16[1280,256]{1,0:T(8,128)(2,1)S(1)} %copy-done), channel_id=1, source_target_pairs={{0,8},{8,0},{16,24},{24,16},{1,9},{9,1},{17,25},{25,17},{2,10},{10... | collective-permute-start | bytes 1966088 | tf_op jit(solution)/shard_map/ppermute | solution.py:29
  1.7 34.1 %collective-permute-start.6 = (bf16[2,16,32,256]{3,2,1,0:T(8,128)(2,1)S(1)}, bf16[2,16,32,256]{3,2,1,0:T(8,128)(2,1)S(1)}, u32[]{:S(2)}, u32[]{:S(2)}) collective-permute-start(bf16[2,16,32,256]{3,2,1,0:T(8,128)(2,1)S(1)} %slice_rows.1), channel_id=1, source_target_pairs={{0,4},{1,5},{2,6},{3,7},{4,0},{5,1},{6,2},{7,3},{8,12},{9,13},{10,... | collective-permute-start | bytes 1572872 | tf_op jit(solution)/shard_map/ppermute | solution.py:29
  5.3 31.7 %collective-permute-start.4 = (bf16[1280,256]{1,0:T(8,128)(2,1)S(1)}, bf16[1280,256]{1,0:T(8,128)(2,1)S(1)}, u32[]{:S(2)}, u32[]{:S(2)}) collective-permute-start(bf16[1280,256]{1,0:T(8,128)(2,1)S(1)} %copy-done), channel_id=1, source_target_pairs={{0,24},{8,16},{16,8},{24,0},{1,25},{9,17},{17,9},{25,1},{2,26},{10... | collective-permute-start | bytes 1966088 | tf_op jit(solution)/shard_map/ppermute | solution.py:29
  6.6 33.4 %collective-permute-start.3 = (bf16[1280,256]{1,0:T(8,128)(2,1)S(1)}, bf16[1280,256]{1,0:T(8,128)(2,1)S(1)}, u32[]{:S(2)}, u32[]{:S(2)}) collective-permute-start(bf16[1280,256]{1,0:T(8,128)(2,1)S(1)} %copy-done), channel_id=1, source_target_pairs={{0,16},{8,24},{16,0},{24,8},{1,17},{9,25},{17,1},{25,9},{2,18},{10... | collective-permute-start | bytes 1966088 | tf_op jit(solution)/shard_map/ppermute | solution.py:29
  9.5 33.9 %copy-start.7 = (bf16[16,16,256]{2,1,0:T(8,128)(2,1)S(1)}, bf16[16,16,256]{2,1,0:T(8,128)(2,1)}, u32[]{:S(2)}) copy-start(bf16[16,16,256]{2,1,0:T(8,128)(2,1)} %get-tuple-element.35) | copy-start | bytes 393220
  9.5 36.1 %copy-start.1 = (bf16[32,16,256]{2,1,0:T(8,128)(2,1)S(1)}, bf16[32,16,256]{2,1,0:T(8,128)(2,1)}, u32[]{:S(2)}) copy-start(bf16[32,16,256]{2,1,0:T(8,128)(2,1)} %get-tuple-element.40.refs_0_) | copy-start | bytes 786436
  9.5 14.1 %collective-permute-start.1 = (bf16[32,16,256]{2,1,0:T(8,128)(2,1)}, bf16[32,16,256]{2,1,0:T(8,128)(2,1)S(1)}, u32[]{:S(2)}, u32[]{:S(2)}) collective-permute-start(bf16[32,16,256]{2,1,0:T(8,128)(2,1)} %get-tuple-element.32), channel_id=1, source_target_pairs={{0,1},{1,0},{2,3},{3,2},{4,5},{5,4},{6,7},{7,6},{8,9},{9,8},{10,11... | collective-permute-start | bytes 786440 | tf_op jit(solution)/shard_map/ppermute | solution.py:29
  11.1 24.7 %collective-permute-start.8 = (bf16[32,16,256]{2,1,0:T(8,128)(2,1)}, bf16[32,16,256]{2,1,0:T(8,128)(2,1)S(1)}, u32[]{:S(2)}, u32[]{:S(2)}) collective-permute-start(bf16[32,16,256]{2,1,0:T(8,128)(2,1)} %get-tuple-element.42), channel_id=1, source_target_pairs={{0,3},{1,2},{2,1},{3,0},{4,7},{5,6},{6,5},{7,4},{8,11},{9,10},{10,... | collective-permute-start | bytes 786440 | tf_op jit(solution)/shard_map/ppermute | solution.py:29
  23.5 19.8 %collective-permute-start.2 = (bf16[32,16,256]{2,1,0:T(8,128)(2,1)}, bf16[32,16,256]{2,1,0:T(8,128)(2,1)S(1)}, u32[]{:S(2)}, u32[]{:S(2)}) collective-permute-start(bf16[32,16,256]{2,1,0:T(8,128)(2,1)} %get-tuple-element.33), channel_id=1, source_target_pairs={{0,6},{1,7},{2,4},{3,5},{4,2},{5,3},{6,0},{7,1},{8,14},{9,15},{10,... | collective-permute-start | bytes 786440 | tf_op jit(solution)/shard_map/ppermute | solution.py:29
  35.8 9.4 %collective-permute-start.9 = (bf16[32,16,256]{2,1,0:T(8,128)(2,1)}, bf16[32,16,256]{2,1,0:T(8,128)(2,1)S(1)}, u32[]{:S(2)}, u32[]{:S(2)}) collective-permute-start(bf16[32,16,256]{2,1,0:T(8,128)(2,1)} %get-tuple-element.43), channel_id=1, source_target_pairs={{0,2},{1,3},{2,0},{3,1},{4,6},{5,7},{6,4},{7,5},{8,10},{9,11},{10,... | collective-permute-start | bytes 786440 | tf_op jit(solution)/shard_map/ppermute | solution.py:29
  35.9 9.7 %collective-permute-start.10 = (bf16[32,16,256]{2,1,0:T(8,128)(2,1)S(1)}, bf16[32,16,256]{2,1,0:T(8,128)(2,1)S(1)}, u32[]{:S(2)}, u32[]{:S(2)}) collective-permute-start(bf16[32,16,256]{2,1,0:T(8,128)(2,1)S(1)} %get-tuple-element.45), channel_id=1, source_target_pairs={{0,1},{1,0},{2,3},{3,2},{4,5},{5,4},{6,7},{7,6},{8,9},{9,8},{10,11... | collective-permute-start | bytes 786440 | tf_op jit(solution)/shard_map/ppermute | solution.py:29
  37.0 9.3 %collective-permute-start.7 = (bf16[16,16,256]{2,1,0:T(8,128)(2,1)}, bf16[16,16,256]{2,1,0:T(8,128)(2,1)S(1)}, u32[]{:S(2)}, u32[]{:S(2)}) collective-permute-start(bf16[16,16,256]{2,1,0:T(8,128)(2,1)} %get-tuple-element.39), channel_id=1, source_target_pairs={{0,7},{1,6},{2,5},{3,4},{4,3},{5,2},{6,1},{7,0},{8,15},{9,14},{10,... | collective-permute-start | bytes 393224 | tf_op jit(solution)/shard_map/ppermute | solution.py:29
  43.4 7.7 %collective-permute-start.5 = (bf16[16,16,256]{2,1,0:T(8,128)(2,1)S(1)}, bf16[16,16,256]{2,1,0:T(8,128)(2,1)S(1)}, u32[]{:S(2)}, u32[]{:S(2)}) collective-permute-start(bf16[16,16,256]{2,1,0:T(8,128)(2,1)S(1)} %copy-done.7), channel_id=1, source_target_pairs={{0,7},{1,6},{2,5},{3,4},{4,3},{5,2},{6,1},{7,0},{8,15},{9,14},{10,... | collective-permute-start | bytes 393224 | tf_op jit(solution)/shard_map/ppermute | solution.py:29
  45.6 0.8 %copy-start.2 = (bf16[128,128]{1,0:T(8,128)(2,1)S(1)}, bf16[128,128]{1,0:T(8,128)(2,1)}, u32[]{:S(2)}) copy-start(bf16[128,128]{1,0:T(8,128)(2,1)} %coupling_ref.3) | copy-start | bytes 98308

commit v4 on v3

--- a/solution.py
+++ b/solution.py
@@ -176,16 +176,16 @@
     half_ref[first : first + rows, pl.ds(pl.multiple_of(own * aux_dev, aux_dev), aux_dev), :] = half
 
 
-def half_kernel(*refs):
-    for k, part_ref in enumerate(refs[:-2]):
+def half_kernel(ways, *refs):
+    for k, part_ref in zip(ways, refs):
         put_half(part_ref[...], k, refs[-2], refs[-1], 0)
 
 
-def half_rows(parts, picked):
+def half_rows(ways, parts, picked):
     slabs, width, occ = picked.shape
     rows, aux_dev, _ = parts[0].shape
     return pl.pallas_call(
-        half_kernel,
+        functools.partial(half_kernel, ways),
         in_specs=[VMEM] * (len(parts) + 1),
         out_specs=VMEM,
         out_shape=pltpu.VMEM((rows, slabs * aux_dev, occ), jnp.bfloat16),
@@ -195,11 +195,11 @@
     )(*parts, picked)
 
 
-def gamma_kernel(first, aliased, last_ref, picked_ref, scaled_ref, coupling_ref, *refs):
+def gamma_kernel(last_way, first, aliased, last_ref, picked_ref, scaled_ref, coupling_ref, *refs):
     half_ref, out_ref, coupled_ref, gamma_ref, sems = refs[aliased:]
     rows, aux_dev, width = last_ref.shape
     slabs, occ, _ = scaled_ref.shape
-    put_half(last_ref[...], slabs - 1, picked_ref, half_ref, first)
+    put_half(last_ref[...], last_way, picked_ref, half_ref, first)
     for m in range(rows):
         half = half_ref[first + m]
         term = jnp.dot(coupling_ref[...], half, preferred_element_type=jnp.float32)
@@ -218,7 +218,7 @@
         copy.wait()
 
 
-def gamma_rows(first, last, picked, scaled, coupling, half, filled=None):
+def gamma_rows(last_way, first, last, picked, scaled, coupling, half, filled=None):
     rows, aux_dev, width = last.shape
     sub, fns, occ = half.shape
     operands = [last, picked, scaled, coupling, half]
@@ -228,7 +228,7 @@
         operands.append(filled)
         in_specs.append(HBM)
     return pl.pallas_call(
-        functools.partial(gamma_kernel, first, len(aliases)),
+        functools.partial(gamma_kernel, last_way, first, len(aliases)),
         in_specs=in_specs,
         out_specs=[VMEM, HBM],
         out_shape=[pltpu.VMEM(half.shape, half.dtype), jax.ShapeDtypeStruct((sub, fns, width), jnp.bfloat16)],
@@ -248,8 +248,9 @@
     slabs = lax.axis_size("aux")
     sub = tiles.shape[1] // slabs
     far, cut = slabs // 2, sub // 2
-    other = [(k, 0, sub) for k in range(far + 2, slabs - 1)]
-    chunks = [(slabs - 1, 0, cut), (slabs - 1, cut, sub - cut)]
+    last = far + 2
+    other = [(k, 0, sub) for k in range(last + 1, slabs)]
+    chunks = [(last, 0, cut), (last, cut, sub - cut)]
     near = [(k, 0, sub) for k in range(far - 1, -1, -1)]
 
     both = slice_rows(pltpu.with_memory_space_constraint(tiles, pltpu.HBM), (far, far + 1), sub)
@@ -270,12 +271,13 @@
         parts[which] = swap(pieces[which], "aux", which[0], *after)
     kept, passed = turn(both)
     parts[far, 0, sub], parts[far + 1, 0, sub] = kept, swap(passed, "aux", 1)
-    early = swap(pieces[chunks[0]], "aux", slabs - 1, both)
-    late = swap(pieces[chunks[1]], "aux", slabs - 1, parts[other[-1]], picked)
-
-    half = half_rows([parts[k, 0, sub] for k in range(slabs - 1)], picked)
-    half, out = gamma_rows(0, early, picked, scaled, coupling, half)
-    return gamma_rows(cut, late, picked, scaled, coupling, half, out)[1]
+    early = swap(pieces[chunks[0]], "aux", last, both)
+    late = swap(pieces[chunks[1]], "aux", last, parts[other[-1]], picked)
+
+    ways = [k for k in range(slabs) if k != last]
+    half = half_rows(ways, [parts[k, 0, sub] for k in ways], picked)
+    half, out = gamma_rows(last, 0, early, picked, scaled, coupling, half)
+    return gamma_rows(last, cut, late, picked, scaled, coupling, half, out)[1]
 
 
 def solution(mesh):

time: 53.5 us -> 52.9 us (0.989)
  waiting for transfers between devices: 25.1 us -> 24.3 us
    ppermute x11, waiting for transfers between devices: 25.1 us -> 24.3 us  [swap(): lax.ppermute(array, axis, [(i, i ^ bit) for i in range(lax.axis_size(axis...]
where the time goes in v4:
time: 52.9 us; the launch traced here: 52.2 us
  waiting for transfers between devices  24.3 us (46%)
  starting transfers between devices  16.4 us (31%)
  Pallas kernels  11.2 us (21%)
    ppermute x11, waiting for transfers between devices, swap(): lax.ppermute(array, axis, [(i, i ^ bit) for i in range(lax.axis_size(axis...  24.3 us
    ppermute x11, starting transfers between devices, swap(): lax.ppermute(array, axis, [(i, i ^ bit) for i in range(lax.axis_size(axis...  16.4 us
    pallas_call x2, Pallas kernels, gamma_rows(): pl.pallas_call(functools.partial(gamma_kernel, last_way, first, len(alias...  3.66 us
    pallas_call x1, Pallas kernels, pick(): pl.pallas_call(functools.partial(pick_kernel, owners), in_specs=[SMEM, VM...  3.29 us
    pallas_call x1, Pallas kernels, cut_rows(): pl.pallas_call(functools.partial(cut_kernel, cuts), in_specs=[HBM], out_s...  2.3 us
    pallas_call x1, Pallas kernels, slice_rows(): pl.pallas_call(functools.partial(slice_kernel, ways), in_specs=[HBM], out...  1.12 us
  transfers between devices with their start and end apart: 11, of which 4 were waited for; matrix products, arithmetic and copies ran while one was open for 0% of the time, Pallas kernels for 16%

profile of v4, /device:TPU:0, one launch (start us, length us, event | category | flops | bytes accessed | tf_op | source)
XLA Modules:
  0.0 52.2 jit_solution(15451943166421211415)
XLA Ops:
  0.0 1.1 %slice_rows.1 = bf16[2,16,32,256]{3,2,1,0:T(8,128)(2,1)S(1)} custom-call(bf16[16,256,256]{2,1,0:T(8,128)(2,1)} %tiles_ref.2), custom_call_target="tpu_custom_call" | custom-call | bytes 1048576 | tf_op jit(solution)/shard_map/slice_rows/pallas_call | solution.py:51
  1.1 0.1 copy-done
  1.2 0.5 collective-permute-start
  1.7 3.6 %collective-permute-start.6 = (bf16[2,16,32,256]{3,2,1,0:T(8,128)(2,1)S(1)}, bf16[2,16,32,256]{3,2,1,0:T(8,128)(2,1)S(1)}, u32[]{:S(2)}, u32[]{:S(2)}) collective-permute-start(bf16[2,16,32,256]{3,2,1,0:T(8,128)(2,1)S(1)} %slice_rows.1), channel_id=1, source_target_pairs={{0,4},{1,5},{2,6},{3,7},{4,0},{5,1},{6,2},{7,3},{8,12},{9,13},{10,... | collective-permute-start | bytes 1572872 | tf_op jit(solution)/shard_map/ppermute | solution.py:29
  5.3 1.3 %collective-permute-start.4 = (bf16[1280,256]{1,0:T(8,128)(2,1)S(1)}, bf16[1280,256]{1,0:T(8,128)(2,1)S(1)}, u32[]{:S(2)}, u32[]{:S(2)}) collective-permute-start(bf16[1280,256]{1,0:T(8,128)(2,1)S(1)} %copy-done), channel_id=1, source_target_pairs={{0,24},{8,16},{16,8},{24,0},{1,25},{9,17},{17,9},{25,1},{2,26},{10... | collective-permute-start | bytes 1966088 | tf_op jit(solution)/shard_map/ppermute | solution.py:29
  6.6 0.5 %collective-permute-start.3 = (bf16[1280,256]{1,0:T(8,128)(2,1)S(1)}, bf16[1280,256]{1,0:T(8,128)(2,1)S(1)}, u32[]{:S(2)}, u32[]{:S(2)}) collective-permute-start(bf16[1280,256]{1,0:T(8,128)(2,1)S(1)} %copy-done), channel_id=1, source_target_pairs={{0,16},{8,24},{16,0},{24,8},{1,17},{9,25},{17,1},{25,9},{2,18},{10... | collective-permute-start | bytes 1966088 | tf_op jit(solution)/shard_map/ppermute | solution.py:29
  7.1 2.3 %cut_rows.1 = (bf16[32,16,256]{2,1,0:T(8,128)(2,1)}, bf16[16,16,256]{2,1,0:T(8,128)(2,1)}, bf16[16,16,256]{2,1,0:T(8,128)(2,1)}, bf16[32,16,256]{2,1,0:T(8,128)(...) custom-call(bf16[16,256,256]{2,1,0:T(8,128)(2,1)} %tiles_ref.2), custom_call_target="tpu_custom_call" | custom-call | bytes 3145728 | tf_op jit(solution)/shard_map/cut_rows/pallas_call | solution.py:102
  9.5 0.0 collective-permute-done.refs_1_
  9.5 1.6 %collective-permute-start.1 = (bf16[32,16,256]{2,1,0:T(8,128)(2,1)}, bf16[32,16,256]{2,1,0:T(8,128)(2,1)S(1)}, u32[]{:S(2)}, u32[]{:S(2)}) collective-permute-start(bf16[32,16,256]{2,1,0:T(8,128)(2,1)} %get-tuple-element.32), channel_id=1, source_target_pairs={{0,1},{1,0},{2,3},{3,2},{4,5},{5,4},{6,7},{7,6},{8,9},{9,8},{10,11... | collective-permute-start | bytes 786440 | tf_op jit(solution)/shard_map/ppermute | solution.py:29
  11.1 1.5 %collective-permute-start.8 = (bf16[32,16,256]{2,1,0:T(8,128)(2,1)}, bf16[32,16,256]{2,1,0:T(8,128)(2,1)S(1)}, u32[]{:S(2)}, u32[]{:S(2)}) collective-permute-start(bf16[32,16,256]{2,1,0:T(8,128)(2,1)} %get-tuple-element.42), channel_id=1, source_target_pairs={{0,3},{1,2},{2,1},{3,0},{4,7},{5,6},{6,5},{7,4},{8,11},{9,10},{10,... | collective-permute-start | bytes 786440 | tf_op jit(solution)/shard_map/ppermute | solution.py:29
  12.6 10.9 %collective-permute-done.1.refs_1_ = bf16[32,16,256]{2,1,0:T(8,128)(2,1)S(1)} collective-permute-done((bf16[32,16,256]{2,1,0:T(8,128)(2,1)}, bf16[32,16,256]{2,1,0:T(8,128)(2,1)S(1)}, u32[]{:S(2)}, u32[]{:S(2)}) %collective-permute-start.1) | collective-permute-done | bytes 262176 | tf_op jit(solution)/shard_map/ppermute | solution.py:29
  23.5 2.4 %collective-permute-start.2 = (bf16[32,16,256]{2,1,0:T(8,128)(2,1)}, bf16[32,16,256]{2,1,0:T(8,128)(2,1)S(1)}, u32[]{:S(2)}, u32[]{:S(2)}) collective-permute-start(bf16[32,16,256]{2,1,0:T(8,128)(2,1)} %get-tuple-element.33), channel_id=1, source_target_pairs={{0,7},{1,6},{2,5},{3,4},{4,3},{5,2},{6,1},{7,0},{8,15},{9,14},{10,... | collective-permute-start | bytes 786440 | tf_op jit(solution)/shard_map/ppermute | solution.py:29
  26.0 9.8 %collective-permute-done.8.refs_3_ = bf16[32,16,256]{2,1,0:T(8,128)(2,1)S(1)} collective-permute-done((bf16[32,16,256]{2,1,0:T(8,128)(2,1)}, bf16[32,16,256]{2,1,0:T(8,128)(2,1)S(1)}, u32[]{:S(2)}, u32[]{:S(2)}) %collective-permute-start.8) | collective-permute-done | bytes 262176 | tf_op jit(solution)/shard_map/ppermute | solution.py:29
  35.8 0.1 turn.1
  35.9 1.1 %collective-permute-start.10 = (bf16[32,16,256]{2,1,0:T(8,128)(2,1)S(1)}, bf16[32,16,256]{2,1,0:T(8,128)(2,1)S(1)}, u32[]{:S(2)}, u32[]{:S(2)}) collective-permute-start(bf16[32,16,256]{2,1,0:T(8,128)(2,1)S(1)} %get-tuple-element.45), channel_id=1, source_target_pairs={{0,1},{1,0},{2,3},{3,2},{4,5},{5,4},{6,7},{7,6},{8,9},{9,8},{10,11... | collective-permute-start | bytes 786440 | tf_op jit(solution)/shard_map/ppermute | solution.py:29
  37.0 3.1 %collective-permute-start.7 = (bf16[16,16,256]{2,1,0:T(8,128)(2,1)}, bf16[16,16,256]{2,1,0:T(8,128)(2,1)S(1)}, u32[]{:S(2)}, u32[]{:S(2)}) collective-permute-start(bf16[16,16,256]{2,1,0:T(8,128)(2,1)} %get-tuple-element.39), channel_id=1, source_target_pairs={{0,6},{1,7},{2,4},{3,5},{4,2},{5,3},{6,0},{7,1},{8,14},{9,15},{10,... | collective-permute-start | bytes 393224 | tf_op jit(solution)/shard_map/ppermute | solution.py:29
  40.1 3.3 %pick_and_scale.1 = (bf16[8,256,256]{2,1,0:T(8,128)(2,1)S(1)}, bf16[8,256,256]{2,1,0:T(8,128)(2,1)S(1)}) custom-call(s32[1,2,8]{2,1,0:T(2,128)S(1)} %bitcast.2, f32[1,256]{1,0:T(1,128)S(1)} %bitcast.3, f32[2]{0:T(128)S(1)} %copy-done.5, f32[2]{0:T(128)S(1)} %copy-done.6, bf16[1280,256]{1,0:T(8,128)(2,1)S(1)} %copy-done, ...), custom_call_target="tpu_custom_call" | custom-call | flops 524288 | bytes 3145728 | tf_op jit(solution)/shard_map/pick_and_scale/pallas_call | solution.py:156
  43.4 0.8 %collective-permute-start.5 = (bf16[16,16,256]{2,1,0:T(8,128)(2,1)S(1)}, bf16[16,16,256]{2,1,0:T(8,128)(2,1)S(1)}, u32[]{:S(2)}, u32[]{:S(2)}) collective-permute-start(bf16[16,16,256]{2,1,0:T(8,128)(2,1)S(1)} %copy-done.7), channel_id=1, source_target_pairs={{0,6},{1,7},{2,4},{3,5},{4,2},{5,3},{6,0},{7,1},{8,14},{9,15},{10,... | collective-permute-start | bytes 393224 | tf_op jit(solution)/shard_map/ppermute | solution.py:29
  44.2 0.9 %collective-permute-done.9.refs_2_ = bf16[32,16,256]{2,1,0:T(8,128)(2,1)S(1)} collective-permute-done((bf16[32,16,256]{2,1,0:T(8,128)(2,1)}, bf16[32,16,256]{2,1,0:T(8,128)(2,1)S(1)}, u32[]{:S(2)}, u32[]{:S(2)}) %collective-permute-start.9) | collective-permute-done | bytes 262176 | tf_op jit(solution)/shard_map/ppermute | solution.py:29
  45.2 0.7 %half_rows.1.refs_0_ = bf16[32,128,256]{2,1,0:T(8,128)(2,1)S(1)} custom-call(bf16[32,16,256]{2,1,0:T(8,128)(2,1)S(1)} %copy-done.1, bf16[32,16,256]{2,1,0:T(8,128)(2,1)S(1)} %collective-permute-done.1.refs_1_, bf16[32,16,256]{2,1,0:T(8,128)(2,1)S(1)} %collective-permute-done.9.refs_2_, bf16[32,16,256]{2,1,0:T(8,128)(2,1)S(1)} %collective-permute-done.8.refs_3_, ...), custom_call_target="tpu_custom_call" | custom-call | flops 469762048 | bytes 3670016 | tf_op jit(solution)/shard_map/half_rows/pallas_call | solution.py:187
  45.9 0.0 copy-done.2
  45.9 1.8 %gamma_rows.2 = (bf16[32,128,256]{2,1,0:T(8,128)(2,1)S(1)}, bf16[32,128,256]{2,1,0:T(8,128)(2,1)}) custom-call(bf16[16,16,256]{2,1,0:T(8,128)(2,1)S(1)} %collective-permute-done.7.last_ref, bf16[8,256,256]{2,1,0:T(8,128)(2,1)S(1)} %get-tuple-element.34.refs_7_.picked_ref, ...), custom_call_target="tpu_custom_call", output_to_operand_aliasing={{0}: (4, {})} | custom-call | flops 402653184 | bytes 6291456 | tf_op jit(solution)/shard_map/gamma_rows/pallas_call | solution.py:230
  47.8 2.6 %collective-permute-done.5.last_ref = bf16[16,16,256]{2,1,0:T(8,128)(2,1)S(1)} collective-permute-done((bf16[16,16,256]{2,1,0:T(8,128)(2,1)S(1)}, bf16[16,16,256]{2,1,0:T(8,128)(2,1)S(1)}, u32[]{:S(2)}, u32[]{:S(2)}) %collective-permute-start.5) | collective-permute-done | bytes 131104 | tf_op jit(solution)/shard_map/ppermute | solution.py:29
  50.4 1.8 %gamma_rows.3 = (bf16[32,128,256]{2,1,0:T(8,128)(2,1)S(1)}, bf16[32,128,256]{2,1,0:T(8,128)(2,1)}) custom-call(bf16[16,16,256]{2,1,0:T(8,128)(2,1)S(1)} %collective-permute-done.5.last_ref, bf16[8,256,256]{2,1,0:T(8,128)(2,1)S(1)} %get-tuple-element.34.refs_7_.picked_ref, ...), custom_call_target="tpu_custom_call", output_to_operand_aliasing={{0}: (4, {}), {1}: (5, {})} | custom-call | flops 402653184 | bytes 6291456 | tf_op jit(solution)/shard_map/gamma_rows/pallas_call | solution.py:230
  (21 shorter events, 0.0 us)
Async XLA Ops:
  0.0 1.2 %copy-start = (bf16[1280,256]{1,0:T(8,128)(2,1)S(1)}, bf16[1280,256]{1,0:T(8,128)(2,1)}, u32[]{:S(2)}) copy-start(bf16[1280,256]{1,0:T(8,128)(2,1)} %refs_0_) | copy-start | bytes 1966084
  0.0 40.1 %copy-start.6 = (f32[2]{0:T(128)S(1)}, f32[2]{0:T(128)}, u32[]{:S(2)}) copy-start(f32[2]{0:T(128)} %weights_ref.1) | copy-start | bytes 28
  0.0 40.1 %copy-start.5 = (f32[2]{0:T(128)S(1)}, f32[2]{0:T(128)}, u32[]{:S(2)}) copy-start(f32[2]{0:T(128)} %tau_ref.1) | copy-start | bytes 28
  0.0 40.1 %copy-start.4 = (f32[256]{0:T(256)S(1)}, f32[256]{0:T(256)}, u32[]{:S(2)}) copy-start(f32[256]{0:T(256)} %param.10) | copy-start | bytes 3076
  0.0 40.1 %copy-start.3 = (s32[1,8,2]{1,2,0:T(2,128)S(1)}, s32[1,8,2]{1,2,0:T(2,128)}, u32[]{:S(2)}) copy-start(s32[1,8,2]{1,2,0:T(2,128)} %param.8) | copy-start | bytes 196
  1.2 8.2 %collective-permute-start = (bf16[1280,256]{1,0:T(8,128)(2,1)S(1)}, bf16[1280,256]{1,0:T(8,128)(2,1)S(1)}, u32[]{:S(2)}, u32[]{:S(2)}) collective-permute-start(bf16[1280,256]{1,0:T(8,128)(2,1)S(1)} %copy-done), channel_id=1, source_target_pairs={{0,8},{8,0},{16,24},{24,16},{1,9},{9,1},{17,25},{25,17},{2,10},{10... | collective-permute-start | bytes 1966088 | tf_op jit(solution)/shard_map/ppermute | solution.py:29
  1.7 34.1 %collective-permute-start.6 = (bf16[2,16,32,256]{3,2,1,0:T(8,128)(2,1)S(1)}, bf16[2,16,32,256]{3,2,1,0:T(8,128)(2,1)S(1)}, u32[]{:S(2)}, u32[]{:S(2)}) collective-permute-start(bf16[2,16,32,256]{3,2,1,0:T(8,128)(2,1)S(1)} %slice_rows.1), channel_id=1, source_target_pairs={{0,4},{1,5},{2,6},{3,7},{4,0},{5,1},{6,2},{7,3},{8,12},{9,13},{10,... | collective-permute-start | bytes 1572872 | tf_op jit(solution)/shard_map/ppermute | solution.py:29
  5.3 31.7 %collective-permute-start.4 = (bf16[1280,256]{1,0:T(8,128)(2,1)S(1)}, bf16[1280,256]{1,0:T(8,128)(2,1)S(1)}, u32[]{:S(2)}, u32[]{:S(2)}) collective-permute-start(bf16[1280,256]{1,0:T(8,128)(2,1)S(1)} %copy-done), channel_id=1, source_target_pairs={{0,24},{8,16},{16,8},{24,0},{1,25},{9,17},{17,9},{25,1},{2,26},{10... | collective-permute-start | bytes 1966088 | tf_op jit(solution)/shard_map/ppermute | solution.py:29
  6.6 33.5 %collective-permute-start.3 = (bf16[1280,256]{1,0:T(8,128)(2,1)S(1)}, bf16[1280,256]{1,0:T(8,128)(2,1)S(1)}, u32[]{:S(2)}, u32[]{:S(2)}) collective-permute-start(bf16[1280,256]{1,0:T(8,128)(2,1)S(1)} %copy-done), channel_id=1, source_target_pairs={{0,16},{8,24},{16,0},{24,8},{1,17},{9,25},{17,1},{25,9},{2,18},{10... | collective-permute-start | bytes 1966088 | tf_op jit(solution)/shard_map/ppermute | solution.py:29
  9.5 34.0 %copy-start.7 = (bf16[16,16,256]{2,1,0:T(8,128)(2,1)S(1)}, bf16[16,16,256]{2,1,0:T(8,128)(2,1)}, u32[]{:S(2)}) copy-start(bf16[16,16,256]{2,1,0:T(8,128)(2,1)} %get-tuple-element.35) | copy-start | bytes 393220
  9.5 35.7 %copy-start.1 = (bf16[32,16,256]{2,1,0:T(8,128)(2,1)S(1)}, bf16[32,16,256]{2,1,0:T(8,128)(2,1)}, u32[]{:S(2)}) copy-start(bf16[32,16,256]{2,1,0:T(8,128)(2,1)} %get-tuple-element.40.refs_0_) | copy-start | bytes 786436
  9.5 14.1 %collective-permute-start.1 = (bf16[32,16,256]{2,1,0:T(8,128)(2,1)}, bf16[32,16,256]{2,1,0:T(8,128)(2,1)S(1)}, u32[]{:S(2)}, u32[]{:S(2)}) collective-permute-start(bf16[32,16,256]{2,1,0:T(8,128)(2,1)} %get-tuple-element.32), channel_id=1, source_target_pairs={{0,1},{1,0},{2,3},{3,2},{4,5},{5,4},{6,7},{7,6},{8,9},{9,8},{10,11... | collective-permute-start | bytes 786440 | tf_op jit(solution)/shard_map/ppermute | solution.py:29
  11.1 24.7 %collective-permute-start.8 = (bf16[32,16,256]{2,1,0:T(8,128)(2,1)}, bf16[32,16,256]{2,1,0:T(8,128)(2,1)S(1)}, u32[]{:S(2)}, u32[]{:S(2)}) collective-permute-start(bf16[32,16,256]{2,1,0:T(8,128)(2,1)} %get-tuple-element.42), channel_id=1, source_target_pairs={{0,3},{1,2},{2,1},{3,0},{4,7},{5,6},{6,5},{7,4},{8,11},{9,10},{10,... | collective-permute-start | bytes 786440 | tf_op jit(solution)/shard_map/ppermute | solution.py:29
  23.5 19.9 %collective-permute-start.2 = (bf16[32,16,256]{2,1,0:T(8,128)(2,1)}, bf16[32,16,256]{2,1,0:T(8,128)(2,1)S(1)}, u32[]{:S(2)}, u32[]{:S(2)}) collective-permute-start(bf16[32,16,256]{2,1,0:T(8,128)(2,1)} %get-tuple-element.33), channel_id=1, source_target_pairs={{0,7},{1,6},{2,5},{3,4},{4,3},{5,2},{6,1},{7,0},{8,15},{9,14},{10,... | collective-permute-start | bytes 786440 | tf_op jit(solution)/shard_map/ppermute | solution.py:29
  35.8 9.4 %collective-permute-start.9 = (bf16[32,16,256]{2,1,0:T(8,128)(2,1)}, bf16[32,16,256]{2,1,0:T(8,128)(2,1)S(1)}, u32[]{:S(2)}, u32[]{:S(2)}) collective-permute-start(bf16[32,16,256]{2,1,0:T(8,128)(2,1)} %get-tuple-element.43), channel_id=1, source_target_pairs={{0,2},{1,3},{2,0},{3,1},{4,6},{5,7},{6,4},{7,5},{8,10},{9,11},{10,... | collective-permute-start | bytes 786440 | tf_op jit(solution)/shard_map/ppermute | solution.py:29
  35.9 9.3 %collective-permute-start.10 = (bf16[32,16,256]{2,1,0:T(8,128)(2,1)S(1)}, bf16[32,16,256]{2,1,0:T(8,128)(2,1)S(1)}, u32[]{:S(2)}, u32[]{:S(2)}) collective-permute-start(bf16[32,16,256]{2,1,0:T(8,128)(2,1)S(1)} %get-tuple-element.45), channel_id=1, source_target_pairs={{0,1},{1,0},{2,3},{3,2},{4,5},{5,4},{6,7},{7,6},{8,9},{9,8},{10,11... | collective-permute-start | bytes 786440 | tf_op jit(solution)/shard_map/ppermute | solution.py:29
  37.0 8.9 %collective-permute-start.7 = (bf16[16,16,256]{2,1,0:T(8,128)(2,1)}, bf16[16,16,256]{2,1,0:T(8,128)(2,1)S(1)}, u32[]{:S(2)}, u32[]{:S(2)}) collective-permute-start(bf16[16,16,256]{2,1,0:T(8,128)(2,1)} %get-tuple-element.39), channel_id=1, source_target_pairs={{0,6},{1,7},{2,4},{3,5},{4,2},{5,3},{6,0},{7,1},{8,14},{9,15},{10,... | collective-permute-start | bytes 393224 | tf_op jit(solution)/shard_map/ppermute | solution.py:29
  43.4 6.9 %collective-permute-start.5 = (bf16[16,16,256]{2,1,0:T(8,128)(2,1)S(1)}, bf16[16,16,256]{2,1,0:T(8,128)(2,1)S(1)}, u32[]{:S(2)}, u32[]{:S(2)}) collective-permute-start(bf16[16,16,256]{2,1,0:T(8,128)(2,1)S(1)} %copy-done.7), channel_id=1, source_target_pairs={{0,6},{1,7},{2,4},{3,5},{4,2},{5,3},{6,0},{7,1},{8,14},{9,15},{10,... | collective-permute-start | bytes 393224 | tf_op jit(solution)/shard_map/ppermute | solution.py:29
  45.2 0.8 %copy-start.2 = (bf16[128,128]{1,0:T(8,128)(2,1)S(1)}, bf16[128,128]{1,0:T(8,128)(2,1)}, u32[]{:S(2)}) copy-start(bf16[128,128]{1,0:T(8,128)(2,1)} %coupling_ref.3) | copy-start | bytes 98308
